TPU v7x, 256 devices: a whole 4x4x8 slice. The times are simulated.
256 devices in a mesh: qrow: 16 (over x, z_hi, core), kcol: 16 (over y, z_lo).
Axes of the slice: x: 4, y: 4, z: 8 (z_hi: 2, z_lo: 4; z = z_hi * 4 + z_lo), core: 2. Of those that a mesh axis runs over, the one named last changes fastest.
Arguments:
- query: bfloat16 [32768, 512], P(('qrow', 'kcol')), may hold values from -6 to 6
- keys: bfloat16 [32768, 128], P(('kcol', 'qrow')), may hold values from -6 to 6
- values: bfloat16 [32768, 128], P(('kcol', 'qrow')), may hold values from -6 to 6
- out: bfloat16 [32768, 512], P(('qrow', 'kcol')), may hold values from -6 to 6
- out_grad: bfloat16 [32768, 512], P(('qrow', 'kcol')), may hold values from -0.59765625 to 0.59765625
- lse: float32 [4, 32768], P(None, ('qrow', 'kcol')), may hold values from 2.5 to 4.5
- cu_seqlens: int32 [7], replicated, may hold values from 0 to 32768, as said below
- tile_table: int32 [16, 16, 16], P('qrow', 'kcol'), may hold values from -1 to 15, as said below
Outputs:
- query_grad: bfloat16 [32768, 512], P(('qrow', 'kcol'))
- key_grad: bfloat16 [32768, 128], P(('kcol', 'qrow'))
- value_grad: bfloat16 [32768, 128], P(('kcol', 'qrow'))
Inputs may be any that keep to these rules, and one draw needn't show every extreme that they name: cu_seqlens[0] = 0, cu_seqlens[6] = 32768, rising; every document holds 1024 to 16384 tokens, one exactly 1024 and one exactly 16384. tile_table[i, j] holds, in rising order, the codes of exactly those tiles of device (i, j) that contain a query row and a key row whose positions lie in one document with the key's position not after the query's, then -1 in the remaining entries.
All inputs are finite; a program needn't handle non-finite values.
Results may differ from a plain program's by a relative error of at most 0.0049.
Values may be sent and summed in bfloat16 or wider, within the bound.
A program may use at most 64 MiB of HBM per device.

v0:
```python
import math

import jax
import jax.numpy as jnp
from jax import lax
from jax.sharding import PartitionSpec as P

HEADS = 4
HEAD_DIM = 128
TILE = 512


def doc_of(positions, cu_seqlens):
    inner = cu_seqlens[1:-1]
    return jnp.sum((inner[None, :] <= positions[:, None]).astype(jnp.int32), axis=1)


def row_deltas(out_rows, grad_rows):
    row_count = out_rows.shape[0]
    product = out_rows.astype(jnp.float32) * grad_rows.astype(jnp.float32)
    return jnp.sum(product.reshape(row_count, HEADS, HEAD_DIM), axis=2).T


def tile_grads(
    query_tile,
    grad_tile,
    key_tile,
    value_tile,
    lse_tile,
    delta_tile,
    query_pos,
    key_pos,
    cu_seqlens,
):
    row_count = query_tile.shape[0]
    scaling = 1.0 / math.sqrt(HEAD_DIM)
    query_heads = query_tile.reshape(row_count, HEADS, HEAD_DIM)
    grad_heads = grad_tile.reshape(row_count, HEADS, HEAD_DIM)
    scores = (
        jnp.einsum("qhd,kd->hqk", query_heads, key_tile, preferred_element_type=jnp.float32)
        * scaling
    )
    same_doc = doc_of(query_pos, cu_seqlens)[:, None] == doc_of(key_pos, cu_seqlens)[None, :]
    allowed = same_doc & (key_pos[None, :] <= query_pos[:, None])
    weights = jnp.where(allowed[None], jnp.exp(scores - lse_tile[:, :, None]), jnp.float32(0.0))
    weights_low = weights.astype(jnp.bfloat16)
    dprobs = jnp.einsum("qhd,kd->hqk", grad_heads, value_tile, preferred_element_type=jnp.float32)
    dscores = weights * (dprobs - delta_tile[:, :, None])
    dscores_low = dscores.astype(jnp.bfloat16)
    value_part = jnp.einsum(
        "hqk,qhd->kd", weights_low, grad_heads, preferred_element_type=jnp.float32
    )
    key_part = (
        jnp.einsum("hqk,qhd->kd", dscores_low, query_heads, preferred_element_type=jnp.float32)
        * scaling
    )
    query_part = jnp.einsum(
        "hqk,kd->qhd", dscores_low, key_tile, preferred_element_type=jnp.float32
    )
    return (query_part.reshape(row_count, HEADS * HEAD_DIM) * scaling, key_part, value_part)


def per_device(query, keys, values, out, out_grad, lse, cu_seqlens, tile_table):
    query_block, grad_block, out_block = (
        lax.all_gather(query, "kcol", axis=0, tiled=True),
        lax.all_gather(out_grad, "kcol", axis=0, tiled=True),
        lax.all_gather(out, "kcol", axis=0, tiled=True),
    )
    lse_block = lax.all_gather(lse, "kcol", axis=1, tiled=True)
    delta_block = row_deltas(out_block, grad_block)
    key_block, value_block = (
        lax.all_gather(keys, "qrow", axis=0, tiled=True),
        lax.all_gather(values, "qrow", axis=0, tiled=True),
    )
    query_rows = query_block.shape[0]
    key_rows = key_block.shape[0]
    key_tiles = key_rows // TILE
    row_index = lax.axis_index("qrow")
    col_index = lax.axis_index("kcol")
    row_groups = lax.axis_size("qrow")
    col_groups = lax.axis_size("kcol")
    tile_codes = tile_table.reshape(-1)
    start_sums = (
        jnp.zeros((query_rows, HEADS * HEAD_DIM), jnp.float32),
        jnp.zeros((key_rows, HEAD_DIM), jnp.float32),
        jnp.zeros((key_rows, HEAD_DIM), jnp.float32),
    )

    def visit(number, totals):
        tile_code = tile_codes[number]

        def work(sums):
            query_sum, key_sum, value_sum = sums
            q_tile = tile_code // key_tiles
            k_tile = tile_code % key_tiles
            q_start = q_tile * TILE
            k_start = k_tile * TILE
            query_pos = (q_tile * row_groups + row_index) * TILE + jnp.arange(TILE, dtype=jnp.int32)
            key_pos = (k_tile * col_groups + col_index) * TILE + jnp.arange(TILE, dtype=jnp.int32)
            query_part, key_part, value_part = tile_grads(
                lax.dynamic_slice_in_dim(query_block, q_start, TILE, 0),
                lax.dynamic_slice_in_dim(grad_block, q_start, TILE, 0),
                lax.dynamic_slice_in_dim(key_block, k_start, TILE, 0),
                lax.dynamic_slice_in_dim(value_block, k_start, TILE, 0),
                lax.dynamic_slice_in_dim(lse_block, q_start, TILE, 1),
                lax.dynamic_slice_in_dim(delta_block, q_start, TILE, 1),
                query_pos,
                key_pos,
                cu_seqlens,
            )
            query_sum = lax.dynamic_update_slice_in_dim(
                query_sum,
                lax.dynamic_slice_in_dim(query_sum, q_start, TILE, 0) + query_part,
                q_start,
                0,
            )
            key_sum = lax.dynamic_update_slice_in_dim(
                key_sum, lax.dynamic_slice_in_dim(key_sum, k_start, TILE, 0) + key_part, k_start, 0
            )
            value_sum = lax.dynamic_update_slice_in_dim(
                value_sum,
                lax.dynamic_slice_in_dim(value_sum, k_start, TILE, 0) + value_part,
                k_start,
                0,
            )
            return (query_sum, key_sum, value_sum)

        return lax.cond(tile_code >= 0, work, lambda sums: sums, totals)

    query_sum, key_sum, value_sum = lax.fori_loop(0, tile_codes.shape[0], visit, start_sums)
    query_grad = lax.psum_scatter(query_sum, "kcol", scatter_dimension=0, tiled=True).astype(
        jnp.bfloat16
    )
    key_grad, value_grad = (
        lax.psum_scatter(key_sum, "qrow", scatter_dimension=0, tiled=True),
        lax.psum_scatter(value_sum, "qrow", scatter_dimension=0, tiled=True),
    )
    return (query_grad, key_grad.astype(jnp.bfloat16), value_grad.astype(jnp.bfloat16))


def solution(mesh):
    placed = (
        P(("qrow", "kcol"), None),
        P(("kcol", "qrow"), None),
        P(("kcol", "qrow"), None),
        P(("qrow", "kcol"), None),
        P(("qrow", "kcol"), None),
        P(None, ("qrow", "kcol")),
        P(),
        P("qrow", "kcol", None),
    )
    return jax.shard_map(
        per_device,
        mesh=mesh,
        in_specs=placed,
        out_specs=(P(("qrow", "kcol"), None), P(("kcol", "qrow"), None), P(("kcol", "qrow"), None)),
        check_vma=False,
    )
```

profile of v0, /device:TPU:33, one launch (start us, length us, event | category | flops | bytes accessed | tf_op | source)
XLA Modules:
  0.0 641.3 jit_solution(1520212504094898788)
XLA Ops:
  7.2 1.7 copy.32
  8.9 1.7 copy.31
  10.7 1.7 copy.30
  12.4 32.2 %all_gather.20 = f32[4,2048]{1,0:T(4,128)S(1)} all-gather(f32[4,128]{1,0:T(4,128)} %param.17), channel_id=1, replica_groups=mesh['qrow'=16,'kcol'=16] {'kcol'}, dimensions={1}, use_global_device_ids=true | all-gather | bytes 34816 | tf_op jit(solution)/shard_map/all_gather | solution.py:69
  44.7 45.3 %all_gather.18 = bf16[2048,128]{1,0:T(8,128)(2,1)S(1)} all-gather(bf16[128,128]{1,0:T(8,128)(2,1)} %param.13), channel_id=1, replica_groups=mesh['qrow'=16,'kcol'=16] {'qrow'}, dimensions={0}, use_global_device_ids=true | all-gather | bytes 557056 | tf_op jit(solution)/shard_map/all_gather | solution.py:72
  89.9 31.6 %all_gather.21 = bf16[2048,128]{1,0:T(8,128)(2,1)S(1)} all-gather(bf16[128,128]{1,0:T(8,128)(2,1)} %param.14), channel_id=1, replica_groups=mesh['qrow'=16,'kcol'=16] {'qrow'}, dimensions={0}, use_global_device_ids=true | all-gather | bytes 557056 | tf_op jit(solution)/shard_map/all_gather | solution.py:73
  121.5 62.2 %all-gather.6.cloned.1.call-done = bf16[2048,512]{0,1:T(8,128)(2,1)} async-done(((bf16[128,512]{0,1:T(8,128)(2,1)}), bf16[2048,512]{0,1:T(8,128)(2,1)}) %all-gather.6.cloned.1.call-update) | async-done | bytes 2097168 | tf_op jit(solution)/shard_map/all_gather | solution.py:66
  183.8 2.9 bitcast_reduce_fusion
  186.7 83.2 %all-gather.4.cloned.1.call-done = bf16[2048,512]{0,1:T(8,128)(2,1)} async-done(((bf16[128,512]{0,1:T(8,128)(2,1)}), bf16[2048,512]{0,1:T(8,128)(2,1)}) %all-gather.4.cloned.1.call-update) | async-done | bytes 2097168 | tf_op jit(solution)/shard_map/all_gather | solution.py:65
  270.0 2.5 broadcast_in_dim.10
  272.5 76.7 %while.17 = (s32[]{:T(128)}, f32[2048,512]{0,1:T(8,128)}, f32[2048,128]{1,0:T(8,128)S(1)}, f32[2048,128]{1,0:T(8,128)S(1)}, s32[16]{0:T(128)S(1)}, /*index=5*/bf...) while((s32[]{:T(128)}, f32[2048,512]{0,1:T(8,128)}, ...), condition=%wide.region_6.7_spmd, body=%wide.region_1.6_spmd.sunk | while | flops 1354185728 | bytes 29569820 | solution.py:130
  273.7 11.3 %conditional.2 = ((f32[2048,512]{0,1:T(8,128)}, f32[2048,128]{1,0:T(8,128)S(1)}, f32[2048,128]{1,0:T(8,128)S(1)})) conditional(s32[]{:T(128)} %convert_element_type.55, (f32[2048,512]{0,1:T(8,128)}, f32[2048,128]{1,0:T(8,128)S(1)}, f32[2048,128]{1,0:T(8,128)S(1)}) %tuple.45, (s32[]{:T(128)}, f32[2048,512]{0,1:T(8,128)}, ...), branch_computations={%region_2.0_spmd, %region_3.5_spmd} | conditional | flops 1354185728 | bytes 29569508 | solution.py:128
  276.9 1.3 constant_dynamic-slice_fusion.1
  278.1 0.7 fusion.21
  278.8 1.0 fusion.17
  279.9 1.5 fusion.1
  281.4 0.7 fusion.13
  282.6 2.4 constant_dynamic-update-slice_fusion
  286.3 11.3 %conditional.2 = ((f32[2048,512]{0,1:T(8,128)}, f32[2048,128]{1,0:T(8,128)S(1)}, f32[2048,128]{1,0:T(8,128)S(1)})) conditional(s32[]{:T(128)} %convert_element_type.55, (f32[2048,512]{0,1:T(8,128)}, f32[2048,128]{1,0:T(8,128)S(1)}, f32[2048,128]{1,0:T(8,128)S(1)}) %tuple.45, (s32[]{:T(128)}, f32[2048,512]{0,1:T(8,128)}, ...), branch_computations={%region_2.0_spmd, %region_3.5_spmd} | conditional | flops 1354185728 | bytes 29569508 | solution.py:128
  289.4 1.3 constant_dynamic-slice_fusion.1
  290.6 0.7 fusion.21
  291.3 1.0 fusion.17
  292.4 1.5 fusion.1
  293.9 0.7 fusion.13
  295.1 2.4 constant_dynamic-update-slice_fusion
  298.8 11.3 %conditional.2 = ((f32[2048,512]{0,1:T(8,128)}, f32[2048,128]{1,0:T(8,128)S(1)}, f32[2048,128]{1,0:T(8,128)S(1)})) conditional(s32[]{:T(128)} %convert_element_type.55, (f32[2048,512]{0,1:T(8,128)}, f32[2048,128]{1,0:T(8,128)S(1)}, f32[2048,128]{1,0:T(8,128)S(1)}) %tuple.45, (s32[]{:T(128)}, f32[2048,512]{0,1:T(8,128)}, ...), branch_computations={%region_2.0_spmd, %region_3.5_spmd} | conditional | flops 1354185728 | bytes 29569508 | solution.py:128
  301.9 1.3 constant_dynamic-slice_fusion.1
  303.2 0.7 fusion.21
  303.9 1.0 fusion.17
  304.9 1.5 fusion.1
  306.4 0.7 fusion.13
  307.6 2.4 constant_dynamic-update-slice_fusion
  311.3 11.3 %conditional.2 = ((f32[2048,512]{0,1:T(8,128)}, f32[2048,128]{1,0:T(8,128)S(1)}, f32[2048,128]{1,0:T(8,128)S(1)})) conditional(s32[]{:T(128)} %convert_element_type.55, (f32[2048,512]{0,1:T(8,128)}, f32[2048,128]{1,0:T(8,128)S(1)}, f32[2048,128]{1,0:T(8,128)S(1)}) %tuple.45, (s32[]{:T(128)}, f32[2048,512]{0,1:T(8,128)}, ...), branch_computations={%region_2.0_spmd, %region_3.5_spmd} | conditional | flops 1354185728 | bytes 29569508 | solution.py:128
  314.4 1.3 constant_dynamic-slice_fusion.1
  315.7 0.7 fusion.21
  316.4 1.0 fusion.17
  317.4 1.5 fusion.1
  319.0 0.7 fusion.13
  320.2 2.5 constant_dynamic-update-slice_fusion
  323.9 11.3 %conditional.2 = ((f32[2048,512]{0,1:T(8,128)}, f32[2048,128]{1,0:T(8,128)S(1)}, f32[2048,128]{1,0:T(8,128)S(1)})) conditional(s32[]{:T(128)} %convert_element_type.55, (f32[2048,512]{0,1:T(8,128)}, f32[2048,128]{1,0:T(8,128)S(1)}, f32[2048,128]{1,0:T(8,128)S(1)}) %tuple.45, (s32[]{:T(128)}, f32[2048,512]{0,1:T(8,128)}, ...), branch_computations={%region_2.0_spmd, %region_3.5_spmd} | conditional | flops 1354185728 | bytes 29569508 | solution.py:128
  327.0 1.3 constant_dynamic-slice_fusion.1
  328.3 0.7 fusion.21
  329.0 1.0 fusion.17
  330.0 1.5 fusion.1
  331.6 0.7 fusion.13
  332.8 2.5 constant_dynamic-update-slice_fusion
  336.5 0.6 dynamic_slice.54
  337.8 0.6 dynamic_slice.54
  339.1 0.6 dynamic_slice.54
  340.3 0.6 dynamic_slice.54
  341.6 0.6 dynamic_slice.54
  342.9 0.6 dynamic_slice.54
  344.2 0.6 dynamic_slice.54
  345.4 0.6 dynamic_slice.54
  346.7 0.6 dynamic_slice.54
  348.0 0.6 dynamic_slice.54
  349.3 0.9 copy-done.1
  350.9 5.4 copy.33
  356.3 97.1 %reduce-scatter.8.cloned.1.call-done = f32[128,128]{1,0:T(8,128)} async-done(((f32[2048,128]{1,0:T(8,128)}), f32[128,128]{1,0:T(8,128)}) %reduce-scatter.8.cloned.1.call-update) | async-done | bytes 65552 | tf_op jit(solution)/shard_map/reduce_scatter | solution.py:136
  453.4 1.5 convert_element_type.38
  454.8 78.9 %reduce-scatter.6.cloned.1.call-done = f32[128,128]{1,0:T(8,128)} async-done(((f32[2048,128]{1,0:T(8,128)}), f32[128,128]{1,0:T(8,128)}) %reduce-scatter.6.cloned.1.call-update) | async-done | bytes 65552 | tf_op jit(solution)/shard_map/reduce_scatter | solution.py:135
  533.7 1.5 convert_element_type.37
  535.2 97.7 %reduce-scatter.4.cloned.1.call-done = f32[128,512]{1,0:T(8,128)} async-done(((f32[2048,512]{1,0:T(8,128)}), f32[128,512]{1,0:T(8,128)}) %reduce-scatter.4.cloned.1.call-update) | async-done | bytes 262160 | tf_op jit(solution)/shard_map/reduce_scatter | solution.py:131
  632.8 1.6 convert_element_type.36
  (69 shorter events, 9.3 us)
Async XLA Ops:
  7.2 114.4 %all-gather.8.cloned.1.call-start = ((), (), s32[]{:S(2)}) async-start(), calls=%async_computation.5 | async-start | bytes 2228224 | tf_op jit(solution)/shard_map/all_gather | solution.py:67
  8.9 174.9 %all-gather.6.cloned.1.call-start = ((), (), s32[]{:S(2)}) async-start(), calls=%async_computation.4 | async-start | bytes 2228224 | tf_op jit(solution)/shard_map/all_gather | solution.py:66
  10.6 259.2 %all-gather.4.cloned.1.call-start = ((), (), s32[]{:S(2)}) async-start(), calls=%async_computation.3 | async-start | bytes 2228224 | tf_op jit(solution)/shard_map/all_gather | solution.py:65
  12.4 441.0 %reduce-scatter.8.cloned.1.call-start = ((), (), s32[]{:S(2)}) async-start(), calls=%async_computation.8 | async-start | bytes 1114112 | tf_op jit(solution)/shard_map/reduce_scatter | solution.py:136
  186.7 85.8 %copy-start.2 = (s32[1,1,16]{2,1,0:T(1,128)S(1)}, s32[1,1,16]{2,1,0:T(1,128)}, u32[]{:S(2)}) copy-start(s32[1,1,16]{2,1,0:T(1,128)} %param.19) | copy-start | bytes 196
  186.7 85.8 %copy-start.3 = (s32[7]{0:T(128)S(1)}, s32[7]{0:T(128)}, u32[]{:S(2)}) copy-start(s32[7]{0:T(128)} %param.18) | copy-start | bytes 88
  349.2 1.0 copy-start.1
  349.3 1.4 copy-start
  350.2 183.5 %reduce-scatter.6.cloned.1.call-start = ((), (), s32[]{:S(2)}) async-start(), calls=%async_computation.7 | async-start | bytes 1114112 | tf_op jit(solution)/shard_map/reduce_scatter | solution.py:135
  350.8 282.0 %reduce-scatter.4.cloned.1.call-start = ((), (), s32[]{:S(2)}) async-start(), calls=%async_computation.6 | async-start | bytes 4456448 | tf_op jit(solution)/shard_map/reduce_scatter | solution.py:131
Sparse Core Ops, SparseCore 0:
  9.7 84.4 all-gather.7
  95.9 87.8 all-gather.5
  186.1 83.7 all-gather.3
  350.4 102.9 reduce-scatter.7
  457.9 75.7 reduce-scatter.5
  536.1 96.6 reduce-scatter.3
where the time goes:
time: 649 us; the launch traced here: 641 us
  waiting for transfers between devices  419 us (65%)
  blocking collectives  109 us (17%)
  local copies, waits for them, and re-layouts  30.5 us (5%)
  loops' own time  24.3 us (4%)
  matrix products  22.2 us (3%)
  other arithmetic  21.5 us (3%)
  between operations  14.2 us (2%)
    reduce_scatter x1, waiting for transfers between devices, per_device(): lax.psum_scatter(query_sum, 'kcol', scatter_dimension=0, tiled=True)  97.7 us
    reduce_scatter x1, waiting for transfers between devices, per_device(): lax.psum_scatter(value_sum, 'qrow', scatter_dimension=0, tiled=True)  97.1 us
    all_gather x1, waiting for transfers between devices, per_device(): lax.all_gather(query, 'kcol', axis=0, tiled=True)  83.2 us
    reduce_scatter x1, waiting for transfers between devices, per_device(): lax.psum_scatter(key_sum, 'qrow', scatter_dimension=0, tiled=True)  78.9 us
    all_gather x1, waiting for transfers between devices, per_device(): lax.all_gather(out_grad, 'kcol', axis=0, tiled=True)  62.2 us
    all_gather x1, blocking collectives, per_device(): lax.all_gather(keys, 'qrow', axis=0, tiled=True)  45.3 us
    all_gather x1, blocking collectives, per_device(): lse_block = lax.all_gather(lse, 'kcol', axis=1, tiled=True)  32.2 us
    all_gather x1, blocking collectives, per_device(): lax.all_gather(values, 'qrow', axis=0, tiled=True)  31.6 us
  transfers between devices with their start and end apart: 6, of which 5 were waited for; matrix products, arithmetic and copies ran while one was open for 2% of the time, Pallas kernels for 0%

commit v1 on v0

v1 whole, which is shorter than its diff:
```python
import functools
import math

import jax
import jax.numpy as jnp
from jax import lax
from jax.experimental import pallas as pl
from jax.experimental.pallas import tpu as pltpu
from jax.sharding import PartitionSpec as P

MESH = pl.DeviceIdType.MESH
HEADS = 4
HEAD_DIM = 128
TILE = 512
SUB = 128
SCALE = 1.0 / math.sqrt(HEAD_DIM)
LOG2E = math.log2(math.e)
LANE = (((1,), (1,)), ((), ()))
ROW = (((0,), (0,)), ((), ()))
COLS = HEADS * SUB


def compute_kernel(
    cu_ref, q_ref, g_ref, st_ref, k_ref, v_ref, dq_ref, dk_ref, dv_ref, qh, gh, lse, delta, dqa, dka, dva
):
    row = lax.axis_index("qrow")
    col = lax.axis_index("kcol")
    y = col // 4
    part = col % 4
    for a in range(4):
        for h in range(HEADS):
            lanes = slice(h * SUB, (h + 1) * SUB)
            qh[a, lanes, :] = q_ref[a, :, lanes]
            gh[a, lanes, :] = g_ref[a, :, lanes]
            lse[a, :, lanes] = st_ref[a, h : h + 1, :]
            delta[a, :, lanes] = st_ref[a, HEADS + h : HEADS + h + 1, :]
    dka[...] = jnp.zeros_like(dka)
    dva[...] = jnp.zeros_like(dva)
    dqa[...] = jnp.zeros_like(dqa)

    def doc_start(pos):
        start = jnp.int32(0)
        for n in range(1, 6):
            start = jnp.where(cu_ref[n] <= pos, cu_ref[n], start)
        return start

    def tiles_before(tile):
        return tile // 16 * 4 + jnp.clip(tile % 16 - 4 * y, 0, 4)

    def query_part(a, carry):
        tile = a * 16 + row
        first = tile * TILE + part * SUB
        start = doc_start(first)
        last_start = doc_start(first + SUB - 1)
        low = tiles_before(start // TILE)
        high = tiles_before(tile + 1)
        qpos = first + lax.broadcasted_iota(jnp.int32, (1, SUB), 1)
        starts = jnp.zeros((1, SUB), jnp.int32)
        for n in range(1, 6):
            starts = jnp.where(cu_ref[n] <= qpos, cu_ref[n], starts)

        def unit(kt, masked):
            base = (kt // 4 * 16 + 4 * y + kt % 4) * TILE
            for part_k in range(2):
                rows = slice(part_k * 256, (part_k + 1) * 256)
                keys = k_ref[kt, rows, :]
                vals = v_ref[kt, rows, :]
                scores = lax.dot_general(keys, qh[a], LANE, preferred_element_type=jnp.float32)
                weights = jnp.exp2(scores * (SCALE * LOG2E) - lse[a])
                if masked:
                    kpos = base + part_k * 256 + lax.broadcasted_iota(jnp.int32, (256, SUB), 0)
                    allowed = (kpos >= starts) & (kpos <= qpos)
                    weights = jnp.concatenate(
                        [
                            jnp.where(allowed, weights[:, h * SUB : (h + 1) * SUB], 0.0)
                            for h in range(HEADS)
                        ],
                        axis=1,
                    )
                probs = lax.dot_general(vals, gh[a], LANE, preferred_element_type=jnp.float32)
                dscores = (weights * (probs - delta[a])).astype(jnp.bfloat16)
                dva[kt, rows, :] += jnp.dot(
                    weights.astype(jnp.bfloat16), gh[a], preferred_element_type=jnp.float32
                )
                dka[kt, rows, :] += jnp.dot(dscores, qh[a], preferred_element_type=jnp.float32)
                dqa[a] += lax.dot_general(dscores, keys, ROW, preferred_element_type=jnp.float32)

        def visit(kt, carry):
            base = (kt // 4 * 16 + 4 * y + kt % 4) * TILE
            full = (base + TILE - 1 <= first) & (last_start <= base)

            @pl.when(full)
            def _():
                unit(kt, False)

            @pl.when(jnp.logical_not(full))
            def _():
                unit(kt, True)

            return carry

        lax.fori_loop(low, high, visit, 0)
        return carry

    lax.fori_loop(0, 4, query_part, 0)
    for a in range(4):
        for h in range(HEADS):
            lanes = slice(h * SUB, (h + 1) * SUB)
            dq_ref[a, :, lanes] = (dqa[a, lanes, :] * SCALE).astype(jnp.bfloat16)

    def finish(kt, carry):
        dk_ref[kt] = (dka[kt] * SCALE).astype(jnp.bfloat16)
        dv_ref[kt] = dva[kt].astype(jnp.bfloat16)
        return carry

    lax.fori_loop(0, 16, finish, 0)


def compute(cu, q, g, st, k, v):
    vmem = pl.BlockSpec(memory_space=pltpu.VMEM)
    return pl.pallas_call(
        compute_kernel,
        out_shape=[
            jax.ShapeDtypeStruct((4, SUB, COLS), jnp.bfloat16),
            jax.ShapeDtypeStruct((16, TILE, HEAD_DIM), jnp.bfloat16),
            jax.ShapeDtypeStruct((16, TILE, HEAD_DIM), jnp.bfloat16),
        ],
        in_specs=[pl.BlockSpec(memory_space=pltpu.SMEM)] + [vmem] * 5,
        out_specs=[vmem] * 3,
        scratch_shapes=[
            pltpu.VMEM((4, COLS, HEAD_DIM), jnp.bfloat16),
            pltpu.VMEM((4, COLS, HEAD_DIM), jnp.bfloat16),
            pltpu.VMEM((4, 1, COLS), jnp.float32),
            pltpu.VMEM((4, 1, COLS), jnp.float32),
            pltpu.VMEM((4, COLS, HEAD_DIM), jnp.float32),
            pltpu.VMEM((16, TILE, HEAD_DIM), jnp.float32),
            pltpu.VMEM((16, TILE, HEAD_DIM), jnp.float32),
        ],
        compiler_params=pltpu.CompilerParams(vmem_limit_bytes=56 * 1024 * 1024),
        name="tiles",
    )(cu, q, g, st, k, v)


class Place:
    def __init__(self):
        row = lax.axis_index("qrow")
        col = lax.axis_index("kcol")
        self.x = row // 4
        self.core = row % 2
        self.y = col // 4
        self.z = row // 2 % 2 * 4 + col % 4

    def at(self, dx=0, dy=0, dz=0, flip=0):
        x = (self.x + dx + 4) % 4
        y = (self.y + dy + 4) % 4
        z = (self.z + dz + 8) % 8
        core = 1 - self.core if flip else self.core
        return (x * 4 + z // 4 * 2 + core, y * 4 + z % 4)

    def xs(self, dx):
        return (self.x + dx + 4) % 4

    def ys(self, dy):
        return (self.y + dy + 4) % 4

    def zs(self, dz):
        z = (self.z + dz + 8) % 8
        return z % 4 * 2 + z // 4


class Sender:
    def __init__(self, send_sem, recv_sem):
        self.send_sem = send_sem
        self.recv_sem = recv_sem
        self.sent = []

    def start(self, src, dst, device):
        number = len(self.sent)
        copy = pltpu.make_async_remote_copy(
            src_ref=src,
            dst_ref=dst,
            send_sem=self.send_sem.at[number],
            recv_sem=self.recv_sem.at[number],
            device_id=device,
            device_id_type=MESH,
        )
        copy.start()
        self.sent.append(copy)
        return copy

    def finish(self):
        for copy in self.sent:
            copy.wait_send()


def greet(devices):
    barrier = pltpu.get_barrier_semaphore()
    for device in devices:
        pl.semaphore_signal(barrier, inc=1, device_id=device, device_id_type=MESH)
    pl.semaphore_wait(barrier, len(devices))


GATHER_COPIES = 72
REDUCE_COPIES = 56


def gather_kernel(
    q_ref, g_ref, k_ref, v_ref, o_ref, lse_ref, qa, ga, ka, va, sta, stats, send_sem, recv_sem, own_sem
):
    me = Place()
    x, y, core = me.x, me.y, me.core
    greet(
        [
            me.at(dx=1),
            me.at(dx=2),
            me.at(dx=3),
            me.at(dy=1),
            me.at(dy=2),
            me.at(dy=3),
            me.at(dz=1),
            me.at(dz=-1),
            me.at(flip=1),
        ]
    )
    net = Sender(send_sem, recv_sem)
    here = me.zs(0)
    own = [
        pltpu.make_async_copy(k_ref, ka.at[x, here, core], own_sem.at[0]),
        pltpu.make_async_copy(v_ref, va.at[x, here, core], own_sem.at[1]),
        pltpu.make_async_copy(q_ref, qa.at[y], own_sem.at[2]),
        pltpu.make_async_copy(g_ref, ga.at[y], own_sem.at[3]),
    ]
    for copy in own:
        copy.start()

    v_up = [net.start(v_ref, va.at[x, here, core], me.at(dz=1))]
    v_down = [net.start(v_ref, va.at[x, here, core], me.at(dz=-1))]
    k_side = [net.start(k_ref, ka.at[x, here, core], me.at(dx=d)) for d in (1, 3, 2)]
    q_up = net.start(q_ref, qa.at[y], me.at(dy=1))
    g_down = net.start(g_ref, ga.at[y], me.at(dy=-1))
    q_down = net.start(q_ref, qa.at[y], me.at(dy=-1))
    g_up = net.start(g_ref, ga.at[y], me.at(dy=1))
    v_side = []
    v_far = []

    def spread(dz):
        slot = me.zs(dz)
        block = va.at[x, slot, core]
        v_side.append((dz, net.start(block, block, me.at(dx=1)), net.start(block, block, me.at(dx=-1))))

    def spread_far(number):
        dz, up, down = v_side[number]
        slot = me.zs(dz)
        up.wait_recv()
        down.wait_recv()
        if number % 2 == 0:
            block = va.at[me.xs(-1), slot, core]
            v_far.append(net.start(block, block, me.at(dx=1)))
        else:
            block = va.at[me.xs(1), slot, core]
            v_far.append(net.start(block, block, me.at(dx=-1)))

    for copy in own:
        copy.wait()
    spread(0)

    for h in range(HEADS):
        lanes = slice(h * SUB, (h + 1) * SUB)
        product = o_ref[:, lanes].astype(jnp.float32) * g_ref[:, lanes].astype(jnp.float32)
        stats[HEADS + h : HEADS + h + 1, :] = jnp.sum(product.T, axis=0, keepdims=True)
    stats[0:HEADS, :] = lse_ref[...] * LOG2E
    stat_own = pltpu.make_async_copy(stats, sta.at[y], own_sem.at[4])
    stat_own.start()
    stat_side = [net.start(stats, sta.at[y], me.at(dy=d)) for d in (1, 2, 3)]

    sibling = me.at(flip=1)
    mirrored = []

    def mirror(block):
        mirrored.append(net.start(block, block, sibling))

    def v_step(step):
        v_up[-1].wait_recv()
        v_down[-1].wait_recv()
        if step < 3:
            up = va.at[x, me.zs(-step), core]
            down = va.at[x, me.zs(step), core]
            v_up.append(net.start(up, up, me.at(dz=1)))
            v_down.append(net.start(down, down, me.at(dz=-1)))
        elif step == 3:
            up = va.at[x, me.zs(-3), core, 0:64]
            down = va.at[x, me.zs(3), core, 64:128]
            v_up.append(net.start(up, up, me.at(dz=1)))
            v_down.append(net.start(down, down, me.at(dz=-1)))
        if step < 4:
            spread(-step)
            spread(step)
        else:
            spread(4)

    v_step(1)
    for copy in k_side:
        copy.wait_recv()
    bundle = ka.at[:, here, core]
    k_up = [net.start(bundle, bundle, me.at(dz=1))]
    k_down = [net.start(bundle, bundle, me.at(dz=-1))]
    mirror(bundle)

    def k_step(step):
        k_up[-1].wait_recv()
        k_down[-1].wait_recv()
        if step < 3:
            up = ka.at[:, me.zs(-step), core]
            down = ka.at[:, me.zs(step), core]
            k_up.append(net.start(up, up, me.at(dz=1)))
            k_down.append(net.start(down, down, me.at(dz=-1)))
            mirror(up)
            mirror(down)
        elif step == 3:
            up = ka.at[0:2, me.zs(-3), core]
            down = ka.at[2:4, me.zs(3), core]
            k_up.append(net.start(up, up, me.at(dz=1)))
            k_down.append(net.start(down, down, me.at(dz=-1)))
            mirror(ka.at[:, me.zs(-3), core])
            mirror(ka.at[:, me.zs(3), core])
        else:
            mirror(ka.at[:, me.zs(4), core])

    v_step(2)
    q_up.wait_recv()
    block = qa.at[me.ys(-1)]
    q_far = net.start(block, block, me.at(dy=1))
    g_down.wait_recv()
    block = ga.at[me.ys(1)]
    g_far = net.start(block, block, me.at(dy=-1))
    v_step(3)
    k_step(1)
    spread_far(0)
    spread_far(1)
    spread_far(2)
    v_step(4)
    mirror(va.at[x, :, core])
    k_step(2)
    spread_far(3)
    spread_far(4)
    spread_far(5)
    k_step(3)
    spread_far(6)
    spread_far(7)
    mirror(va.at[me.xs(1), :, core])
    mirror(va.at[me.xs(-1), :, core])
    k_step(4)
    for copy in v_far:
        copy.wait_recv()
    mirror(va.at[me.xs(2), :, core])
    for copy in [q_down, g_up, q_far, g_far] + stat_side + mirrored:
        copy.wait_recv()
    stat_own.wait()
    net.finish()


def gather(q, g, k, v, o, lse):
    vmem = pl.BlockSpec(memory_space=pltpu.VMEM)
    anywhere = pl.BlockSpec(memory_space=pl.ANY)
    return pl.pallas_call(
        gather_kernel,
        out_shape=[
            jax.ShapeDtypeStruct((4, SUB, COLS), jnp.bfloat16),
            jax.ShapeDtypeStruct((4, SUB, COLS), jnp.bfloat16),
            jax.ShapeDtypeStruct((4, 8, 2, SUB, HEAD_DIM), jnp.bfloat16),
            jax.ShapeDtypeStruct((4, 8, 2, SUB, HEAD_DIM), jnp.bfloat16),
            jax.ShapeDtypeStruct((4, 2 * HEADS, SUB), jnp.float32),
        ],
        in_specs=[vmem] * 6,
        out_specs=[anywhere] * 5,
        scratch_shapes=[
            pltpu.VMEM((2 * HEADS, SUB), jnp.float32),
            pltpu.SemaphoreType.DMA((GATHER_COPIES,)),
            pltpu.SemaphoreType.DMA((GATHER_COPIES,)),
            pltpu.SemaphoreType.DMA((5,)),
        ],
        compiler_params=pltpu.CompilerParams(
            collective_id=0, has_side_effects=True, vmem_limit_bytes=16 * 1024 * 1024
        ),
        name="gather",
    )(q, g, k, v, o, lse)


def reduce_kernel(
    dq_ref,
    dk_ref,
    dv_ref,
    dq_out,
    dk_out,
    dv_out,
    k_own,
    v_own,
    k_in,
    v_in,
    q_in,
    kx_send,
    kx_in,
    kz_send,
    kz_in,
    vz_send,
    vz_in,
    vx_send,
    vx_in,
    q_own,
    send_sem,
    recv_sem,
    own_sem,
):
    me = Place()
    x, y, core = me.x, me.y, me.core
    other = 1 - core
    sibling = me.at(flip=1)
    own = [
        pltpu.make_async_copy(dk_ref.at[:, :, core], k_own, own_sem.at[0]),
        pltpu.make_async_copy(dv_ref.at[:, :, core], v_own, own_sem.at[1]),
        pltpu.make_async_copy(dq_ref.at[y], q_own, own_sem.at[2]),
    ]
    for copy in own:
        copy.start()
    peers = [me.at(dx=d) for d in (1, 2, 3)] + [me.at(dy=d) for d in (1, 2, 3)]
    peers += [me.at(dz=d) for d in range(1, 8)] + [sibling]
    greet(peers)
    net = Sender(send_sem, recv_sem)
    f32 = jnp.float32
    bf16 = jnp.bfloat16

    v_pair = {}
    k_pair = {}

    def pair_v(dz):
        v_pair[dz] = net.start(dv_ref.at[:, me.zs(dz), other], v_in.at[:, me.zs(dz)], sibling)

    def pair_k(dx):
        k_pair[dx] = net.start(dk_ref.at[me.xs(dx), :, other], k_in.at[me.xs(dx)], sibling)

    pair_v(4)
    pair_k(2)
    pair_v(3)
    pair_v(-3)
    pair_k(1)
    pair_v(2)
    pair_v(-2)
    pair_k(-1)
    pair_v(1)
    pair_v(-1)
    pair_k(0)
    pair_v(0)
    q_side = [net.start(dq_ref.at[me.ys(d)], q_in.at[d - 1], me.at(dy=d)) for d in (1, 3, 2)]
    for copy in own:
        copy.wait()

    def v_sum(dz, rows):
        slot = me.zs(dz)
        return v_own[rows, slot].astype(f32) + v_in[rows, slot].astype(f32)

    def k_sum(dx, rows):
        slot = me.xs(dx)
        return k_own[slot, rows].astype(f32) + k_in[slot, rows].astype(f32)

    low, high, both = slice(0, 2), slice(2, 4), slice(0, 4)
    first, second = slice(0, 4), slice(4, 8)

    v_pair[4].wait_recv()
    vz_send[0, 0, low] = v_sum(4, low).astype(bf16)
    vz_send[1, 0, high] = v_sum(4, high).astype(bf16)
    v_up = [net.start(vz_send.at[0, 0, low], vz_in.at[0, 0, low], me.at(dz=1))]
    v_down = [net.start(vz_send.at[1, 0, high], vz_in.at[1, 0, high], me.at(dz=-1))]

    k_pair[2].wait_recv()
    kx_send[0, 0] = k_sum(2, first).astype(bf16)
    kx_send[1, 0] = k_sum(2, second).astype(bf16)
    kx_up = [net.start(kx_send.at[0, 0], kx_in.at[0, 0], me.at(dx=1))]
    kx_down = [net.start(kx_send.at[1, 0], kx_in.at[1, 0], me.at(dx=-1))]

    def v_step(step):
        dz = 4 - step
        v_pair[dz].wait_recv()
        v_pair[-dz].wait_recv()
        v_up[-1].wait_recv()
        v_down[-1].wait_recv()
        if step == 1:
            vz_send[0, 1, low] = (v_sum(dz, low) + vz_in[0, 0, low].astype(f32)).astype(bf16)
            vz_send[0, 1, high] = v_sum(dz, high).astype(bf16)
            vz_send[1, 1, low] = v_sum(-dz, low).astype(bf16)
            vz_send[1, 1, high] = (v_sum(-dz, high) + vz_in[1, 0, high].astype(f32)).astype(bf16)
        else:
            vz_send[0, step] = (v_sum(dz, both) + vz_in[0, step - 1].astype(f32)).astype(bf16)
            vz_send[1, step] = (v_sum(-dz, both) + vz_in[1, step - 1].astype(f32)).astype(bf16)
        v_up.append(net.start(vz_send.at[0, step], vz_in.at[0, step], me.at(dz=1)))
        v_down.append(net.start(vz_send.at[1, step], vz_in.at[1, step], me.at(dz=-1)))

    k_pair[1].wait_recv()
    k_pair[-1].wait_recv()
    kx_send[0, 1] = k_sum(1, second).astype(bf16)
    kx_send[1, 1] = k_sum(-1, first).astype(bf16)
    kx_up.append(net.start(kx_send.at[0, 1], kx_in.at[0, 1], me.at(dx=1)))
    kx_down.append(net.start(kx_send.at[1, 1], kx_in.at[1, 1], me.at(dx=-1)))
    v_step(1)
    kx_up[0].wait_recv()
    kx_down[0].wait_recv()
    kx_send[0, 2] = (k_sum(1, first) + kx_in[0, 0].astype(f32)).astype(bf16)
    kx_send[1, 2] = (k_sum(-1, second) + kx_in[1, 0].astype(f32)).astype(bf16)
    kx_up.append(net.start(kx_send.at[0, 2], kx_in.at[0, 2], me.at(dx=1)))
    kx_down.append(net.start(kx_send.at[1, 2], kx_in.at[1, 2], me.at(dx=-1)))
    v_step(2)
    v_step(3)

    k_pair[0].wait_recv()
    for copy in (kx_up[1], kx_up[2], kx_down[1], kx_down[2]):
        copy.wait_recv()
    k_total = k_sum(0, first) + kx_in[0, 2].astype(f32) + kx_in[1, 1].astype(f32)
    kz_send[0:4] = k_total.astype(bf16)
    k_total = k_sum(0, second) + kx_in[0, 1].astype(f32) + kx_in[1, 2].astype(f32)
    kz_send[4:8] = k_total.astype(bf16)
    kz = [net.start(kz_send.at[me.zs(d)], kz_in.at[d - 1], me.at(dz=d)) for d in (4, 3, 5, 2, 6, 1, 7)]

    v_pair[0].wait_recv()
    v_up[3].wait_recv()
    v_down[3].wait_recv()
    vx_send[...] = (
        v_sum(0, both) + vz_in[0, 3].astype(f32) + vz_in[1, 3].astype(f32)
    ).astype(bf16)
    vx = [net.start(vx_send.at[me.xs(d)], vx_in.at[d - 1], me.at(dx=d)) for d in (1, 3, 2)]

    for copy in q_side:
        copy.wait_recv()
    total = q_own[...].astype(f32)
    for n in range(3):
        total += q_in[n].astype(f32)
    dq_out[...] = total.astype(bf16)
    for copy in kz:
        copy.wait_recv()
    total = kz_send[me.zs(0)].astype(f32)
    for n in range(7):
        total += kz_in[n].astype(f32)
    dk_out[...] = total.astype(bf16)
    for copy in vx:
        copy.wait_recv()
    total = vx_send[x].astype(f32)
    for n in range(3):
        total += vx_in[n].astype(f32)
    dv_out[...] = total.astype(bf16)
    net.finish()


def reduce(dq, dk, dv):
    vmem = pl.BlockSpec(memory_space=pltpu.VMEM)
    anywhere = pl.BlockSpec(memory_space=pl.ANY)
    bf16 = jnp.bfloat16
    block = (SUB, HEAD_DIM)
    return pl.pallas_call(
        reduce_kernel,
        out_shape=[
            jax.ShapeDtypeStruct((SUB, COLS), bf16),
            jax.ShapeDtypeStruct(block, bf16),
            jax.ShapeDtypeStruct(block, bf16),
        ],
        in_specs=[anywhere] * 3,
        out_specs=[vmem] * 3,
        scratch_shapes=[
            pltpu.VMEM((4, 8) + block, bf16),
            pltpu.VMEM((4, 8) + block, bf16),
            pltpu.VMEM((4, 8) + block, bf16),
            pltpu.VMEM((4, 8) + block, bf16),
            pltpu.VMEM((3, SUB, COLS), bf16),
            pltpu.VMEM((2, 3, 4) + block, bf16),
            pltpu.VMEM((2, 3, 4) + block, bf16),
            pltpu.VMEM((8,) + block, bf16),
            pltpu.VMEM((7,) + block, bf16),
            pltpu.VMEM((2, 4, 4) + block, bf16),
            pltpu.VMEM((2, 4, 4) + block, bf16),
            pltpu.VMEM((4,) + block, bf16),
            pltpu.VMEM((3,) + block, bf16),
            pltpu.VMEM((SUB, COLS), bf16),
            pltpu.SemaphoreType.DMA((REDUCE_COPIES,)),
            pltpu.SemaphoreType.DMA((REDUCE_COPIES,)),
            pltpu.SemaphoreType.DMA((3,)),
        ],
        compiler_params=pltpu.CompilerParams(
            collective_id=1, has_side_effects=True, vmem_limit_bytes=32 * 1024 * 1024
        ),
        name="reduce",
    )(dq, dk, dv)


def per_device(query, keys, values, out, out_grad, lse, cu_seqlens, tile_table):
    q, g, k, v, st = gather(query, out_grad, keys, values, out, lse)
    tiles = (16, TILE, HEAD_DIM)
    dq, dk, dv = compute(cu_seqlens, q, g, st, k.reshape(tiles), v.reshape(tiles))
    blocks = (4, 8, 2, SUB, HEAD_DIM)
    return reduce(dq, dk.reshape(blocks), dv.reshape(blocks))


def solution(mesh):
    placed = (
        P(("qrow", "kcol"), None),
        P(("kcol", "qrow"), None),
        P(("kcol", "qrow"), None),
        P(("qrow", "kcol"), None),
        P(("qrow", "kcol"), None),
        P(None, ("qrow", "kcol")),
        P(),
        P("qrow", "kcol", None),
    )
    return jax.shard_map(
        per_device,
        mesh=mesh,
        in_specs=placed,
        out_specs=(P(("qrow", "kcol"), None), P(("kcol", "qrow"), None), P(("kcol", "qrow"), None)),
        check_vma=False,
    )
```

time: 649 us -> 110 us (0.17)
  the two profiles are of different devices: /device:TPU:33 before, /device:TPU:8 now
where the time goes in v1:
time: 110 us
  Pallas kernels  93.1 us (85%)
  local copies, waits for them, and re-layouts  15.9 us (14%)
    pallas_call x1, Pallas kernels, reduce(): pl.pallas_call(reduce_kernel, out_shape=[jax.ShapeDtypeStruct((SUB, COLS)...  39.2 us
    pallas_call x1, Pallas kernels, gather(): pl.pallas_call(gather_kernel, out_shape=[jax.ShapeDtypeStruct((4, SUB, CO...  35.9 us
    pallas_call x1, Pallas kernels, compute(): pl.pallas_call(compute_kernel, out_shape=[jax.ShapeDtypeStruct((4, SUB, C...  18 us
    unnamed x31, local copies, waits for them, and re-layouts  15.9 us

profile of v1, /device:TPU:8, one launch (start us, length us, event | category | flops | bytes accessed | tf_op | source)
XLA Modules:
  0.0 109.7 jit_solution(14714274705440902735)
XLA Ops:
  0.6 0.0 copy-start.7
  0.6 0.9 copy-done.7
  1.5 0.0 copy-start.8
  1.5 0.9 copy-done.8
  2.4 0.0 copy-start.9
  2.4 0.9 copy-done.9
  3.3 0.0 copy-start.10
  3.3 0.8 copy-done.10
  4.1 0.0 copy-start.11
  4.1 0.8 copy-done.11
  4.9 0.0 copy-start.13
  4.9 0.7 copy-done.13
  5.5 35.9 %gather.1 = (bf16[4,128,512]{2,1,0:T(8,128)(2,1)S(1)}, bf16[4,128,512]{2,1,0:T(8,128)(2,1)S(1)}, bf16[4,8,2,128,128]{4,3,2,1,0:T(8,128)(2,1)S(1)}, bf16[4,8,2,12...) custom-call(bf16[128,512]{1,0:T(8,128)(2,1)S(1)} %copy-done.7, bf16[128,512]{1,0:T(8,128)(2,1)S(1)} %copy-done.8, ...), custom_call_target="tpu_custom_call" | custom-call | tf_op jit(solution)/shard_map/gather/pallas_call | solution.py:365
  41.4 0.0 copy-start.2
  41.4 1.3 %copy-done.2 = bf16[4,8,2,128,128]{4,3,2,1,0:T(8,128)(2,1)} copy-done((bf16[4,8,2,128,128]{4,3,2,1,0:T(8,128)(2,1)}, bf16[4,8,2,128,128]{4,3,2,1,0:T(8,128)(2,1)S(1)}, u32[]{:S(2)}) %copy-start.2) | copy-done | bytes 2097176
  42.8 0.0 copy-start.3
  42.8 1.3 %copy-done.3 = bf16[4,8,2,128,128]{4,3,2,1,0:T(8,128)(2,1)} copy-done((bf16[4,8,2,128,128]{4,3,2,1,0:T(8,128)(2,1)}, bf16[4,8,2,128,128]{4,3,2,1,0:T(8,128)(2,1)S(1)}, u32[]{:S(2)}) %copy-start.3) | copy-done | bytes 2097176
  44.1 0.0 copy-start.5
  44.1 0.8 copy-done.5
  44.9 0.0 copy-start.6
  44.9 0.8 copy-done.6
  45.8 0.0 copy-start.12
  45.8 0.6 copy-done.12
  46.4 18.0 %tiles.1 = (bf16[4,128,512]{2,1,0:T(8,128)(2,1)}, bf16[16,512,128]{2,1,0:T(8,128)(2,1)}, bf16[16,512,128]{2,1,0:T(8,128)(2,1)}) custom-call(s32[7]{0:T(128)} %cu_ref.1, bf16[4,128,512]{2,1,0:T(8,128)(2,1)} %copy-done.5, bf16[4,128,512]{2,1,0:T(8,128)(2,1)} %copy-done.6, f32[4,8,128]{2,1,0:T(8,128)} %copy-done.12, bf16[16,512,128]{2,1,0:T(8,128)(2,1)} %bitcast.6, ...), custom_call_target="tpu_custom_call" | custom-call | tf_op jit(solution)/shard_map/tiles/pallas_call | solution.py:121
  64.3 0.0 copy-start
  64.3 1.6 %copy-done = bf16[16,512,128]{2,1,0:T(8,128)(2,1)S(1)} copy-done((bf16[16,512,128]{2,1,0:T(8,128)(2,1)S(1)}, bf16[16,512,128]{2,1,0:T(8,128)(2,1)}, u32[]{:S(2)}) %copy-start) | copy-done | bytes 2097176
  65.9 0.0 copy-start.1
  65.9 1.6 %copy-done.1 = bf16[16,512,128]{2,1,0:T(8,128)(2,1)S(1)} copy-done((bf16[16,512,128]{2,1,0:T(8,128)(2,1)S(1)}, bf16[16,512,128]{2,1,0:T(8,128)(2,1)}, u32[]{:S(2)}) %copy-start.1) | copy-done | bytes 2097176
  67.5 0.0 copy-start.4
  67.5 1.0 copy-done.4
  68.6 39.2 %reduce.1 = (bf16[128,512]{1,0:T(8,128)(2,1)S(1)}, bf16[128,128]{1,0:T(8,128)(2,1)S(1)}, bf16[128,128]{1,0:T(8,128)(2,1)S(1)}) custom-call(bf16[4,128,512]{2,1,0:T(8,128)(2,1)S(1)} %copy-done.4, bf16[4,8,2,128,128]{4,3,2,1,0:T(8,128)(2,1)S(1)} %bitcast.4, bf16[4,8,2,128,128]{4,3,2,1,0:T(8,128)(2,1)S(1)} %bitcast.5), custom_call_target="tpu_custom_call" | custom-call | tf_op jit(solution)/shard_map/reduce/pallas_call | solution.py:556
  107.8 0.7 copy.13
  108.5 0.6 copy.14
  109.1 0.6 copy.15
Async XLA Ops:
  0.6 0.9 copy-start.7
  1.5 0.9 copy-start.8
  2.4 0.9 copy-start.9
  3.3 0.8 copy-start.10
  4.1 0.8 copy-start.11
  4.9 0.7 copy-start.13
  41.4 1.3 %copy-start.2 = (bf16[4,8,2,128,128]{4,3,2,1,0:T(8,128)(2,1)}, bf16[4,8,2,128,128]{4,3,2,1,0:T(8,128)(2,1)S(1)}, u32[]{:S(2)}) copy-start(bf16[4,8,2,128,128]{4,3,2,1,0:T(8,128)(2,1)S(1)} %get-tuple-element.14) | copy-start | bytes 6291460
  42.8 1.3 %copy-start.3 = (bf16[4,8,2,128,128]{4,3,2,1,0:T(8,128)(2,1)}, bf16[4,8,2,128,128]{4,3,2,1,0:T(8,128)(2,1)S(1)}, u32[]{:S(2)}) copy-start(bf16[4,8,2,128,128]{4,3,2,1,0:T(8,128)(2,1)S(1)} %get-tuple-element.15) | copy-start | bytes 6291460
  44.1 0.8 copy-start.5
  44.9 0.8 copy-start.6
  45.8 0.6 copy-start.12
  64.3 1.6 %copy-start = (bf16[16,512,128]{2,1,0:T(8,128)(2,1)S(1)}, bf16[16,512,128]{2,1,0:T(8,128)(2,1)}, u32[]{:S(2)}) copy-start(bf16[16,512,128]{2,1,0:T(8,128)(2,1)} %get-tuple-element.17) | copy-start | bytes 6291460
  65.9 1.6 %copy-start.1 = (bf16[16,512,128]{2,1,0:T(8,128)(2,1)S(1)}, bf16[16,512,128]{2,1,0:T(8,128)(2,1)}, u32[]{:S(2)}) copy-start(bf16[16,512,128]{2,1,0:T(8,128)(2,1)} %get-tuple-element.18) | copy-start | bytes 6291460
  67.5 1.0 copy-start.4

commit v2 on v0

v2 whole, which is shorter than its diff:
```python
import math

import jax
import jax.numpy as jnp
from jax import lax
from jax.experimental import pallas as pl
from jax.experimental.pallas import tpu as pltpu
from jax.sharding import PartitionSpec as P

MESH = pl.DeviceIdType.MESH
HEADS = 4
HEAD_DIM = 128
TILE = 512
SUB = 128
COLS = HEADS * SUB
TOKENS = 32768
SCALE = 1.0 / math.sqrt(HEAD_DIM)
LOG2E = math.log2(math.e)
LANE = (((1,), (1,)), ((), ()))
ROW = (((0,), (0,)), ((), ()))
BF16 = jnp.bfloat16
F32 = jnp.float32
VMEM = pl.BlockSpec(memory_space=pltpu.VMEM)
ANY = pl.BlockSpec(memory_space=pl.ANY)


class Place:
    def __init__(self):
        row = lax.axis_index("qrow")
        col = lax.axis_index("kcol")
        self.x = row // 4
        self.core = row % 2
        self.y = col // 4
        self.z = row // 2 % 2 * 4 + col % 4

    def at(self, dx=0, dy=0, dz=0, flip=0):
        x = (self.x + dx + 4) % 4
        y = (self.y + dy + 4) % 4
        z = (self.z + dz + 8) % 8
        core = 1 - self.core if flip else self.core
        return (x * 4 + z // 4 * 2 + core, y * 4 + z % 4)

    def xs(self, dx):
        return (self.x + dx + 4) % 4

    def ys(self, dy):
        return (self.y + dy + 4) % 4

    def zs(self, dz):
        z = (self.z + dz + 8) % 8
        return z % 4 * 2 + z // 4


class Sender:
    def __init__(self, send_sem, recv_sem):
        self.send_sem = send_sem
        self.recv_sem = recv_sem
        self.sent = []

    def start(self, src, dst, device):
        number = len(self.sent)
        copy = pltpu.make_async_remote_copy(
            src_ref=src,
            dst_ref=dst,
            send_sem=self.send_sem.at[number],
            recv_sem=self.recv_sem.at[number],
            device_id=device,
            device_id_type=MESH,
        )
        copy.start()
        self.sent.append(copy)
        return copy

    def finish(self):
        for copy in self.sent:
            copy.wait_send()


def greet(devices):
    barrier = pltpu.get_barrier_semaphore()
    for device in devices:
        pl.semaphore_signal(barrier, inc=1, device_id=device, device_id_type=MESH)
    pl.semaphore_wait(barrier, len(devices))


def load(pairs, sems):
    copies = [pltpu.make_async_copy(src, dst, sems.at[n]) for n, (src, dst) in enumerate(pairs)]
    for copy in copies:
        copy.start()
    return copies


def gather_kernel(
    q_ref, g_ref, k_ref, v_ref, o_ref, lse_ref, qa, ga, ka, va, sta, g_in, o_in, lse_in, stats,
    send_q, recv_q, send_s, recv_s, send_m, recv_m, send_b, recv_b, own_sem
):
    me = Place()
    x, y, core = me.x, me.y, me.core
    here = me.zs(0)
    sibling = me.at(flip=1)
    own = load(
        [
            (k_ref, ka.at[x, here]),
            (v_ref, va.at[x, here]),
            (q_ref, qa.at[core, y]),
            (g_ref, ga.at[core, y]),
            (g_ref, g_in),
            (o_ref, o_in),
            (lse_ref, lse_in),
        ],
        own_sem,
    )
    greet(
        [me.at(dx=d) for d in (1, 2, 3)]
        + [me.at(dy=d) for d in (1, 2, 3)]
        + [me.at(dy=d, flip=1) for d in (1, 2, 3)]
        + [me.at(dz=1), me.at(dz=-1), sibling]
    )
    net = Sender(send_b, recv_b)
    rows = Sender(send_q, recv_q)
    small = Sender(send_s, recv_s)
    pair = Sender(send_m, recv_m)
    up = net.start(v_ref, va.at[x, here], me.at(dz=1))
    down = net.start(v_ref, va.at[x, here], me.at(dz=-1))
    k_side = [net.start(k_ref, ka.at[x, here], me.at(dx=d)) for d in (1, 3, 2)]
    v_side = [net.start(v_ref, va.at[x, here], me.at(dx=d)) for d in (1, 3, 2)]
    q_rows = {}
    for d in (1, 3, 2):
        q_rows[d] = (
            rows.start(q_ref, qa.at[core, y], me.at(dy=d)),
            rows.start(g_ref, ga.at[core, y], me.at(dy=d)),
        )
    pair.start(q_ref, qa.at[core, y], sibling)
    pair.start(g_ref, ga.at[core, y], sibling)

    def spread(dz):
        block = va.at[x, me.zs(dz)]
        for d in (1, 3, 2):
            v_side.append(net.start(block, block, me.at(dx=d)))

    def mirror(d):
        slot = me.ys(-d)
        for copy, block in zip(q_rows[d], (qa.at[core, slot], ga.at[core, slot])):
            copy.wait_recv()
            pair.start(block, block, sibling)

    halves = (slice(0, 2), slice(2, 4))
    own[0].wait()
    for copy in k_side:
        copy.wait_recv()
    k_up = []
    k_down = []
    for half in halves:
        block = ka.at[half, here]
        k_up.append(net.start(block, block, me.at(dz=1)))
        k_down.append(net.start(block, block, me.at(dz=-1)))

    def k_step(step):
        for n, half in enumerate(halves):
            if step < 4 or n == 0:
                k_up[n].wait_recv()
            if step < 3 or (step == 3 and n == 0):
                block = ka.at[half, me.zs(-step)]
                k_up[n] = net.start(block, block, me.at(dz=1))
            if step < 4 or n == 1:
                k_down[n].wait_recv()
            if step < 3 or (step == 3 and n == 1):
                block = ka.at[half, me.zs(step)]
                k_down[n] = net.start(block, block, me.at(dz=-1))

    def v_step(up, down, step):
        up.wait_recv()
        down.wait_recv()
        if step < 4:
            part = (slice(0, SUB), slice(0, SUB)) if step < 3 else (slice(0, 64), slice(64, SUB))
            block = va.at[x, me.zs(-step), part[0]]
            up = net.start(block, block, me.at(dz=1))
            block = va.at[x, me.zs(step), part[1]]
            down = net.start(block, block, me.at(dz=-1))
            spread(-step)
            spread(step)
        else:
            spread(4)
        return up, down

    up, down = v_step(up, down, 1)
    for copy in own[4:]:
        copy.wait()
    for h in range(HEADS):
        lanes = slice(h * SUB, (h + 1) * SUB)
        product = o_in[:, lanes].astype(F32) * g_in[:, lanes].astype(F32)
        stats[HEADS + h : HEADS + h + 1, :] = jnp.sum(product.T, axis=0, keepdims=True)
    stats[0:HEADS, :] = lse_in[...]
    stat_own = pltpu.make_async_copy(stats, sta.at[core, y], own_sem.at[7])
    stat_own.start()
    k_step(1)
    up, down = v_step(up, down, 2)
    for d in (1, 3, 2):
        small.start(stats, sta.at[core, y], me.at(dy=d))
        small.start(stats, sta.at[core, y], me.at(dy=d, flip=1))
    small.start(stats, sta.at[core, y], sibling)
    k_step(2)
    up, down = v_step(up, down, 3)
    mirror(1)
    mirror(3)
    k_step(3)
    v_step(up, down, 4)
    mirror(2)
    k_step(4)
    for copy in v_side + small.sent + pair.sent:
        copy.wait_recv()
    own[1].wait()
    own[2].wait()
    own[3].wait()
    stat_own.wait()
    for sender in (net, rows, small, pair):
        sender.finish()


def gather(q, g, k, v, o, lse):
    dma = pltpu.SemaphoreType.DMA
    return pl.pallas_call(
        gather_kernel,
        out_shape=[
            jax.ShapeDtypeStruct((2, 4, SUB, COLS), BF16),
            jax.ShapeDtypeStruct((2, 4, SUB, COLS), BF16),
            jax.ShapeDtypeStruct((4, 8, SUB, HEAD_DIM), BF16),
            jax.ShapeDtypeStruct((4, 8, SUB, HEAD_DIM), BF16),
            jax.ShapeDtypeStruct((2, 4, 2 * HEADS, SUB), F32),
        ],
        in_specs=[ANY] * 6,
        out_specs=[ANY] * 5,
        scratch_shapes=[
            pltpu.VMEM((SUB, COLS), BF16),
            pltpu.VMEM((SUB, COLS), BF16),
            pltpu.VMEM((HEADS, SUB), F32),
            pltpu.VMEM((2 * HEADS, SUB), F32),
            dma((6,)),
            dma((6,)),
            dma((7,)),
            dma((7,)),
            dma((8,)),
            dma((8,)),
            dma((49,)),
            dma((49,)),
            dma((8,)),
        ],
        compiler_params=pltpu.CompilerParams(
            collective_id=0, has_side_effects=True, vmem_limit_bytes=63 * 1024 * 1024
        ),
        name="gather",
    )(q, g, k, v, o, lse)


def tiles_kernel(
    cu_ref, q_hbm, g_hbm, st_hbm, k_hbm, v_hbm, dq_hbm, dk_hbm, dv_hbm, q_ref, g_ref, st_ref, k_ref, v_ref, dq_ref, dk_ref, dv_ref,
    qh, gh, feats, dqa, dka, dva, in_sem, out_sem
):
    row = lax.axis_index("qrow")
    col = lax.axis_index("kcol")
    y = col // 4
    part = col % 4
    core = row % 2
    row0 = row - core
    loads = load([(st_hbm, st_ref), (q_hbm, q_ref), (g_hbm, g_ref), (k_hbm, k_ref), (v_hbm, v_ref)], in_sem)
    lane = lax.broadcasted_iota(jnp.int32, (1, SUB), 1)
    sub = lax.broadcasted_iota(jnp.int32, (SUB, 1), 0)
    low_cu = jnp.zeros((1, SUB), jnp.int32) + TOKENS
    high_cu = jnp.zeros((1, SUB), jnp.int32)
    for n in range(6):
        low_cu = jnp.where(lane == n, cu_ref[n], low_cu)
        high_cu = jnp.where(lane == n, cu_ref[n + 1], high_cu)
    ones = (lane >= 8) & (lane < 11)

    def key_base(kt):
        return (kt // 4 * 16 + 4 * y + kt % 4) * TILE + core * SUB

    def clear(kt, carry):
        dka[kt] = jnp.zeros((2 * SUB, HEAD_DIM), F32)
        dva[kt] = jnp.zeros((2 * SUB, HEAD_DIM), F32)
        for zh in range(2):
            pos = key_base(kt) + zh * 2 * SUB + sub
            feats[kt, zh * SUB : (zh + 1) * SUB, :] = (((pos >= low_cu) & (pos < high_cu)) | ones).astype(F32).astype(BF16)
        return carry

    lax.fori_loop(0, 16, clear, 0)
    dqa[...] = jnp.zeros_like(dqa)

    def pieces(vec):
        out = jnp.zeros((SUB, SUB), F32)
        rest = vec
        for n in range(3):
            piece = rest.astype(BF16).astype(F32)
            rest = rest - piece
            out = jnp.where(lane == 8 + n, piece, out)
        return out

    for copy in loads[:3]:
        copy.wait()

    def stack(a, carry):
        for c in range(2):
            qpos = (a * 16 + row0 + c) * TILE + part * SUB + sub
            inside = (qpos >= low_cu) & (qpos < high_cu)
            doc_feat = jnp.where(inside | (lane >= 6), 0.0, -16384.0)
            stat = st_ref[c, a].T
            for h in range(HEADS):
                lanes = slice(h * SUB, (h + 1) * SUB)
                to = slice(c * COLS + h * SUB, c * COLS + (h + 1) * SUB)
                qh[a, to, 0:128] = q_ref[c, a, :, lanes]
                gh[a, to, 0:128] = g_ref[c, a, :, lanes]
                qh[a, to, 128:256] = (doc_feat + pieces(stat[:, h : h + 1] * (-1.0 / SCALE))).astype(BF16)
                gh[a, to, 128:256] = pieces(-stat[:, HEADS + h : HEADS + h + 1]).astype(BF16)
        return carry

    lax.fori_loop(0, 4, stack, 0)
    for copy in loads[3:]:
        copy.wait()

    def doc_start(pos):
        start = jnp.int32(0)
        for n in range(1, 6):
            start = jnp.where(cu_ref[n] <= pos, cu_ref[n], start)
        return start

    def tiles_before(tile):
        return tile // 16 * 4 + jnp.clip(tile % 16 - 4 * y, 0, 4)

    def query_part(a, carry):
        tile = a * 16 + row0
        first = tile * TILE + part * SUB
        low = tiles_before(doc_start(first) // TILE)
        high = tiles_before(tile + 2)

        def unit(kt, masked):
            keys = k_ref[kt]
            vals = v_ref[kt]
            feat = feats[kt]
            scores = lax.dot_general(
                jnp.concatenate([keys, feat], axis=1), qh[a], LANE, preferred_element_type=F32
            )
            weights = jnp.exp2(scores * (SCALE * LOG2E))
            if masked:
                kpos = lax.broadcasted_iota(jnp.int32, (2 * SUB, SUB), 0)
                kpos = jnp.where(kpos >= SUB, kpos + SUB, kpos) + key_base(kt)
                keep = [kpos <= first + lane, kpos <= first + TILE + lane]
                weights = jnp.concatenate(
                    [
                        jnp.where(keep[n // HEADS], weights[:, n * SUB : (n + 1) * SUB], 0.0)
                        for n in range(2 * HEADS)
                    ],
                    axis=1,
                )
            probs = lax.dot_general(
                jnp.concatenate([vals, feat], axis=1), gh[a], LANE, preferred_element_type=F32
            )
            dscores = (weights * probs).astype(BF16)
            dva[kt] += jnp.dot(weights.astype(BF16), gh[a, :, 0:128], preferred_element_type=F32)
            dka[kt] += jnp.dot(dscores, qh[a, :, 0:128], preferred_element_type=F32)
            dqa[a] += lax.dot_general(keys, dscores, ROW, preferred_element_type=F32)

        def visit(kt, carry):
            full = (kt // 4 * 16 + 4 * y + kt % 4) < tile

            @pl.when(full)
            def _():
                unit(kt, False)

            @pl.when(jnp.logical_not(full))
            def _():
                unit(kt, True)

            return carry

        lax.fori_loop(low, high, visit, 0)
        return carry

    lax.fori_loop(0, 4, query_part, 0)
    stores = []
    for b in range(4):
        rows = pl.ds(4 * b, 4)
        for kt in range(4 * b, 4 * b + 4):
            dk_ref[kt] = (dka[kt] * SCALE).astype(BF16)
            dv_ref[kt] = dva[kt].astype(BF16)
        for src, dst in ((dk_ref, dk_hbm), (dv_ref, dv_hbm)):
            copy = pltpu.make_async_copy(src.at[rows], dst.at[rows], out_sem.at[len(stores)])
            copy.start()
            stores.append(copy)
    for c in range(2):
        for a in range(4):
            for h in range(HEADS):
                lanes = slice(h * SUB, (h + 1) * SUB)
                to = slice(c * COLS + h * SUB, c * COLS + (h + 1) * SUB)
                dq_ref[c, a, :, lanes] = (dqa[a, :, to].T * SCALE).astype(BF16)
        copy = pltpu.make_async_copy(dq_ref.at[c], dq_hbm.at[c], out_sem.at[len(stores)])
        copy.start()
        stores.append(copy)
    for copy in stores:
        copy.wait()


def tiles(cu, q, g, st, k, v):
    keys = (16, 2 * SUB, HEAD_DIM)
    rows = (2, 4, SUB, COLS)
    return pl.pallas_call(
        tiles_kernel,
        out_shape=[
            jax.ShapeDtypeStruct(rows, BF16),
            jax.ShapeDtypeStruct(keys, BF16),
            jax.ShapeDtypeStruct(keys, BF16),
        ],
        in_specs=[pl.BlockSpec(memory_space=pltpu.SMEM)] + [ANY] * 5,
        out_specs=[ANY] * 3,
        scratch_shapes=[
            pltpu.VMEM(rows, BF16),
            pltpu.VMEM(rows, BF16),
            pltpu.VMEM((2, 4, 2 * HEADS, SUB), F32),
            pltpu.VMEM(keys, BF16),
            pltpu.VMEM(keys, BF16),
            pltpu.VMEM(rows, BF16),
            pltpu.VMEM(keys, BF16),
            pltpu.VMEM(keys, BF16),
            pltpu.VMEM((4, 2 * COLS, 256), BF16),
            pltpu.VMEM((4, 2 * COLS, 256), BF16),
            pltpu.VMEM(keys, BF16),
            pltpu.VMEM((4, HEAD_DIM, 2 * COLS), F32),
            pltpu.VMEM(keys, F32),
            pltpu.VMEM(keys, F32),
            pltpu.SemaphoreType.DMA((5,)),
            pltpu.SemaphoreType.DMA((10,)),
        ],
        compiler_params=pltpu.CompilerParams(vmem_limit_bytes=63 * 1024 * 1024),
        name="tiles",
    )(cu, q, g, st, k, v)


def reduce_kernel(
    dq_ref, dk_ref, dv_ref, all_out, k_own, k_side, k_send, k_in, v_own, ring_send, ring_in, last_send, last_in,
    q_own, q_pair, q_send, q_in, send_q, recv_q, send_b, recv_b, own_sem
):
    me = Place()
    x, y, core = me.x, me.y, me.core
    sibling = me.at(flip=1)
    own = load(
        [(dv_ref, v_own), (dk_ref.at[x], k_own), (dq_ref.at[core], q_own)],
        own_sem,
    )
    greet(
        [me.at(dx=d) for d in (1, 2, 3)]
        + [me.at(dy=d) for d in (1, 2, 3)]
        + [me.at(dz=d) for d in range(1, 8)]
        + [sibling]
    )
    net = Sender(send_b, recv_b)
    rows = Sender(send_q, recv_q)
    halves = (slice(0, 2), slice(2, 4))
    parts = (slice(0, 4), slice(4, 8))
    far = me.zs(4)
    up = [[net.start(dv_ref.at[halves[0], far], ring_in.at[0, 0, halves[0]], me.at(dz=1)), None]]
    down = [[None, net.start(dv_ref.at[halves[1], far], ring_in.at[1, 0, halves[1]], me.at(dz=-1))]]
    side = []
    for part in parts:
        for d in (2, 1, 3):
            side.append(net.start(dk_ref.at[me.xs(d), part], k_side.at[d - 1, part], me.at(dx=d)))
    pair = rows.start(dq_ref.at[1 - core], q_pair, sibling)
    own[0].wait()

    def v_step(step):
        up.append([None, None])
        down.append([None, None])
        for n in (1, 0) if step == 1 else (0, 1):
            half = halves[n]
            total = v_own[half, me.zs(4 - step)].astype(F32)
            if up[step - 1][n] is not None:
                up[step - 1][n].wait_recv()
                total += ring_in[0, step - 1, half].astype(F32)
            ring_send[0, step - 1, half] = total.astype(BF16)
            up[step][n] = net.start(
                ring_send.at[0, step - 1, half], ring_in.at[0, step, half], me.at(dz=1)
            )
            n = 1 - n if step == 1 else n
            half = halves[n]
            total = v_own[half, me.zs(step - 4)].astype(F32)
            if down[step - 1][n] is not None:
                down[step - 1][n].wait_recv()
                total += ring_in[1, step - 1, half].astype(F32)
            ring_send[1, step - 1, half] = total.astype(BF16)
            down[step][n] = net.start(
                ring_send.at[1, step - 1, half], ring_in.at[1, step, half], me.at(dz=-1)
            )

    def k_part(n):
        part = parts[n]
        total = k_own[part].astype(F32)
        for m in range(3):
            side[3 * n + m].wait_recv()
        for m in range(3):
            total += k_side[m, part].astype(F32)
        k_send[part] = total.astype(BF16)

    v_step(1)
    own[2].wait()
    pair.wait_recv()
    q_rows = []
    for d in (2, 1, 3):
        slot = me.ys(d)
        q_send[d - 1] = (q_own[slot].astype(F32) + q_pair[slot].astype(F32)).astype(BF16)
        q_rows.append(rows.start(q_send.at[d - 1], q_in.at[d - 1], me.at(dy=d)))
    v_step(2)
    own[1].wait()
    k_part(0)
    v_step(3)
    k_part(1)
    k_last = [
        net.start(k_send.at[me.zs(d)], k_in.at[d - 1], me.at(dz=d)) for d in (4, 3, 5, 2, 6, 1, 7)
    ]
    here = me.zs(0)
    for n, half in enumerate(halves):
        up[3][n].wait_recv()
        down[3][n].wait_recv()
        total = v_own[half, here].astype(F32)
        total += ring_in[0, 3, half].astype(F32) + ring_in[1, 3, half].astype(F32)
        last_send[half] = total.astype(BF16)
    v_last = [net.start(last_send.at[me.xs(d)], last_in.at[d - 1], me.at(dx=d)) for d in (2, 1, 3)]
    total = q_own[y].astype(F32) + q_pair[y].astype(F32)
    for copy in q_rows:
        copy.wait_recv()
    for n in range(3):
        total += q_in[n].astype(F32)
    all_out[:, 0:COLS] = total.astype(BF16)
    for copy in k_last:
        copy.wait_recv()
    total = k_send[here].astype(F32)
    for n in range(7):
        total += k_in[n].astype(F32)
    all_out[:, COLS : COLS + HEAD_DIM] = total.astype(BF16)
    for copy in v_last:
        copy.wait_recv()
    total = last_send[x].astype(F32)
    for n in range(3):
        total += last_in[n].astype(F32)
    all_out[:, COLS + HEAD_DIM : COLS + 2 * HEAD_DIM] = total.astype(BF16)
    net.finish()
    rows.finish()


def reduce(dq, dk, dv):
    block = (SUB, HEAD_DIM)
    dma = pltpu.SemaphoreType.DMA
    return pl.pallas_call(
        reduce_kernel,
        out_shape=jax.ShapeDtypeStruct((SUB, COLS + 2 * HEAD_DIM), BF16),
        in_specs=[ANY] * 3,
        out_specs=VMEM,
        scratch_shapes=[
            pltpu.VMEM((8,) + block, BF16),
            pltpu.VMEM((3, 8) + block, BF16),
            pltpu.VMEM((8,) + block, BF16),
            pltpu.VMEM((7,) + block, BF16),
            pltpu.VMEM((4, 8) + block, BF16),
            pltpu.VMEM((2, 3, 4) + block, BF16),
            pltpu.VMEM((2, 4, 4) + block, BF16),
            pltpu.VMEM((4,) + block, BF16),
            pltpu.VMEM((3,) + block, BF16),
            pltpu.VMEM((4, SUB, COLS), BF16),
            pltpu.VMEM((4, SUB, COLS), BF16),
            pltpu.VMEM((3, SUB, COLS), BF16),
            pltpu.VMEM((3, SUB, COLS), BF16),
            dma((4,)),
            dma((4,)),
            dma((30,)),
            dma((30,)),
            dma((3,)),
        ],
        compiler_params=pltpu.CompilerParams(
            collective_id=1, has_side_effects=True, vmem_limit_bytes=63 * 1024 * 1024
        ),
        name="reduce",
    )(dq, dk, dv)


def split_kernel(all_ref, dq_ref, dk_ref, dv_ref):
    dq_ref[...] = all_ref[:, 0:COLS]
    dk_ref[...] = all_ref[:, COLS : COLS + HEAD_DIM]
    dv_ref[...] = all_ref[:, COLS + HEAD_DIM : COLS + 2 * HEAD_DIM]


def split(grads):
    return pl.pallas_call(
        split_kernel,
        out_shape=[
            jax.ShapeDtypeStruct((SUB, COLS), BF16),
            jax.ShapeDtypeStruct((SUB, HEAD_DIM), BF16),
            jax.ShapeDtypeStruct((SUB, HEAD_DIM), BF16),
        ],
        in_specs=[VMEM],
        out_specs=[VMEM] * 3,
        name="split",
    )(grads)


def per_device(query, keys, values, out, out_grad, lse, cu_seqlens, tile_table):
    q, g, k, v, st = gather(query, out_grad, keys, values, out, lse)
    shape = (16, 2 * SUB, HEAD_DIM)
    dq, dk, dv = tiles(cu_seqlens, q, g, st, k.reshape(shape), v.reshape(shape))
    blocks = (4, 8, SUB, HEAD_DIM)
    return split(reduce(dq, dk.reshape(blocks), dv.reshape(blocks)))


def solution(mesh):
    placed = (
        P(("qrow", "kcol"), None),
        P(("kcol", "qrow"), None),
        P(("kcol", "qrow"), None),
        P(("qrow", "kcol"), None),
        P(("qrow", "kcol"), None),
        P(None, ("qrow", "kcol")),
        P(),
        P("qrow", "kcol", None),
    )
    return jax.shard_map(
        per_device,
        mesh=mesh,
        in_specs=placed,
        out_specs=(P(("qrow", "kcol"), None), P(("kcol", "qrow"), None), P(("kcol", "qrow"), None)),
        check_vma=False,
    )
```

time: 649 us -> 88.3 us (0.14)
  the two profiles are of different devices: /device:TPU:33 before, /device:TPU:16 now
where the time goes in v2:
time: 88.3 us; the launch traced here: 88.2 us
  Pallas kernels  87.5 us (99%)
    pallas_call x1, Pallas kernels, reduce(): pl.pallas_call(reduce_kernel, out_shape=jax.ShapeDtypeStruct((SUB, COLS +...  39.5 us
    pallas_call x1, Pallas kernels, gather(): pl.pallas_call(gather_kernel, out_shape=[jax.ShapeDtypeStruct((2, 4, SUB,...  32.5 us
    pallas_call x1, Pallas kernels, tiles(): pl.pallas_call(tiles_kernel, out_shape=[jax.ShapeDtypeStruct(rows, BF16),...  14 us

profile of v2, /device:TPU:16, one launch (start us, length us, event | category | flops | bytes accessed | tf_op | source)
XLA Modules:
  0.0 88.2 jit_solution(4708895994997473810)
XLA Ops:
  0.6 32.5 %gather.1 = (bf16[2,4,128,512]{3,2,1,0:T(8,128)(2,1)}, bf16[2,4,128,512]{3,2,1,0:T(8,128)(2,1)}, bf16[4,8,128,128]{3,2,1,0:T(8,128)(2,1)}, bf16[4,8,128,128]{3,2,1,0:T(8,128)(2,1)}, f32[2,4,8,128]{3,2,1,0:T(8,128)}) custom-call(bf16[128,512]{1,0:T(8,128)(2,1)} %q_ref.1, bf16[128,512]{1,0:T(8,128)(2,1)} %g_ref.1, bf16[128,128]{1,0:T(8,128)(2,1)} %k_ref.1, ...), custom_call_target="tpu_custom_call" | custom-call | tf_op jit(solution)/shard_map/gather/pallas_call | solution.py:222
  33.1 14.0 %tiles.1 = (bf16[2,4,128,512]{3,2,1,0:T(8,128)(2,1)}, bf16[16,256,128]{2,1,0:T(8,128)(2,1)}, bf16[16,256,128]{2,1,0:T(8,128)(2,1)}) custom-call(s32[7]{0:T(128)} %cu_ref.1, bf16[2,4,128,512]{3,2,1,0:T(8,128)(2,1)} %get-tuple-element.11.q_hbm, bf16[2,4,128,512]{3,2,1,0:T(8,128)(2,1)} %get-tuple-element.12.g_hbm, f32[2,4,8,128]{3,2,1,0:T(8,128)} %get-tuple-element.13.st_hbm, ...), custom_call_target="tpu_custom_call" | custom-call | tf_op jit(solution)/shard_map/tiles/pallas_call | solution.py:405
  47.1 39.5 %reduce.1.all_ref = bf16[128,768]{1,0:T(8,128)(2,1)} custom-call(bf16[2,4,128,512]{3,2,1,0:T(8,128)(2,1)} %get-tuple-element.16.dq_ref, bf16[4,8,128,128]{3,2,1,0:T(8,128)(2,1)} %bitcast.6, bf16[4,8,128,128]{3,2,1,0:T(8,128)(2,1)} %bitcast.7), custom_call_target="tpu_custom_call" | custom-call | tf_op jit(solution)/shard_map/reduce/pallas_call | solution.py:550
  86.6 1.6 %split.1 = (bf16[128,512]{1,0:T(8,128)(2,1)}, bf16[128,128]{1,0:T(8,128)(2,1)}, bf16[128,128]{1,0:T(8,128)(2,1)}) custom-call(bf16[128,768]{1,0:T(8,128)(2,1)} %reduce.1.all_ref), custom_call_target="tpu_custom_call" | custom-call | tf_op jit(solution)/shard_map/split/pallas_call | solution.py:589

commit v3 on v0

v3 whole, which is shorter than its diff:
```python
import math

import jax
import jax.numpy as jnp
from jax import lax
from jax.experimental import pallas as pl
from jax.experimental.pallas import tpu as pltpu
from jax.sharding import PartitionSpec as P

MESH = pl.DeviceIdType.MESH
HEADS = 4
HEAD_DIM = 128
TILE = 512
SUB = 128
COLS = HEADS * SUB
TOKENS = 32768
SCALE = 1.0 / math.sqrt(HEAD_DIM)
LOG2E = math.log2(math.e)
LANE = (((1,), (1,)), ((), ()))
ROW = (((0,), (0,)), ((), ()))
BF16 = jnp.bfloat16
F32 = jnp.float32
VMEM = pl.BlockSpec(memory_space=pltpu.VMEM)
ANY = pl.BlockSpec(memory_space=pl.ANY)


class Place:
    def __init__(self):
        row = lax.axis_index("qrow")
        col = lax.axis_index("kcol")
        self.x = row // 4
        self.core = row % 2
        self.y = col // 4
        self.z = row // 2 % 2 * 4 + col % 4

    def at(self, dx=0, dy=0, dz=0, flip=0):
        x = (self.x + dx + 4) % 4
        y = (self.y + dy + 4) % 4
        z = (self.z + dz + 8) % 8
        core = 1 - self.core if flip else self.core
        return (x * 4 + z // 4 * 2 + core, y * 4 + z % 4)

    def xs(self, dx):
        return (self.x + dx + 4) % 4

    def ys(self, dy):
        return (self.y + dy + 4) % 4

    def zs(self, dz):
        z = (self.z + dz + 8) % 8
        return z % 4 * 2 + z // 4


class Sender:
    def __init__(self, send_sem, recv_sem):
        self.send_sem = send_sem
        self.recv_sem = recv_sem
        self.sent = []

    def start(self, src, dst, device):
        number = len(self.sent)
        copy = pltpu.make_async_remote_copy(
            src_ref=src,
            dst_ref=dst,
            send_sem=self.send_sem.at[number],
            recv_sem=self.recv_sem.at[number],
            device_id=device,
            device_id_type=MESH,
        )
        copy.start()
        self.sent.append(copy)
        return copy

    def finish(self):
        for copy in self.sent:
            copy.wait_send()


def greet(devices):
    barrier = pltpu.get_barrier_semaphore()
    for device in devices:
        pl.semaphore_signal(barrier, inc=1, device_id=device, device_id_type=MESH)
    pl.semaphore_wait(barrier, len(devices))


def load(pairs, sems):
    copies = [pltpu.make_async_copy(src, dst, sems.at[n]) for n, (src, dst) in enumerate(pairs)]
    for copy in copies:
        copy.start()
    return copies


def doc_bounds(cu_ref):
    lane = lax.broadcasted_iota(jnp.int32, (1, SUB), 1)
    low = jnp.zeros((1, SUB), jnp.int32) + TOKENS
    high = jnp.zeros((1, SUB), jnp.int32)
    for n in range(6):
        low = jnp.where(lane == 16 + n, cu_ref[n], low)
        high = jnp.where(lane == 16 + n, cu_ref[n + 1], high)
    return lane, low, high


def pieces(vec):
    out = []
    for n in range(3):
        piece = vec.astype(BF16)
        vec = vec - piece.astype(F32)
        out.append(piece)
    return out


def spot(dz):
    if abs(dz) == 4:
        return 7
    return 0 if dz == 0 else 2 * abs(dz) - (1 if dz > 0 else 0)


class Batch:
    def __init__(self, send_sem, recv_sem):
        self.send_sem = send_sem
        self.recv_sem = recv_sem

    def copy(self, src, dst, device):
        return pltpu.make_async_remote_copy(
            src_ref=src,
            dst_ref=dst,
            send_sem=self.send_sem,
            recv_sem=self.recv_sem,
            device_id=device,
            device_id_type=MESH,
        )

    def start(self, src, dst, device):
        self.copy(src, dst, device).start()


class Lane(Sender):
    def __init__(self, send_sem, recv_sem):
        super().__init__(send_sem, recv_sem)

    def start(self, src, dst, device):
        copy = pltpu.make_async_remote_copy(
            src_ref=src,
            dst_ref=dst,
            send_sem=self.send_sem,
            recv_sem=self.recv_sem.at[len(self.sent)],
            device_id=device,
            device_id_type=MESH,
        )
        copy.start()
        self.sent.append(copy)
        return copy

    def finish(self, whole, device):
        pltpu.make_async_remote_copy(
            src_ref=whole,
            dst_ref=whole,
            send_sem=self.send_sem,
            recv_sem=self.recv_sem.at[0],
            device_id=device,
            device_id_type=MESH,
        ).wait_send()


def grads_kernel(
    cu_ref, q_ref, g_ref, k_ref, v_ref, o_ref, lse_ref, all_out, ka, va, rows_in, mine, qs, gs, o_in, lse_in, feats, acc, dqa,
    stage, side_in, z_send, z_in, kept, dq_low, q_pair, q_send, q_in,
    recv_q, recv_m, recv_v, recv_k, send_x, recv_x, send_k, recv_kx, send_all, own_sem, send_s, recv_s, send_z, recv_z, send_d, recv_d
):
    me = Place()
    x, y, z, core = me.x, me.y, me.z, me.core
    here = me.zs(0)
    sibling = me.at(flip=1)
    own = load(
        [
            (k_ref, ka.at[x, here]),
            (v_ref, va.at[x, 0]),
            (q_ref, mine.at[0:SUB]),
            (g_ref, mine.at[SUB : 2 * SUB]),
            (o_ref, o_in),
            (lse_ref, lse_in),
        ],
        own_sem,
    )
    greet(
        [me.at(dx=d) for d in (1, 2, 3)]
        + [me.at(dy=d) for d in (1, 2, 3)]
        + [me.at(dz=d) for d in range(1, 8)]
        + [sibling]
    )
    rows = Lane(send_all.at[0], recv_q)
    pair = Lane(send_all.at[1], recv_m)
    v_ring = Lane(send_all.at[2], recv_v)
    k_ring = Lane(send_all.at[3], recv_k)
    k_cross = Sender(send_k, recv_kx)
    cross = {(d, n): Batch(send_x.at[d - 1, n], recv_x.at[d - 1, n]) for d in (1, 2, 3) for n in range(5)}
    k_side = [k_cross.start(k_ref, ka.at[x, here], me.at(dx=d)) for d in (2, 1, 3)]
    up = v_ring.start(v_ref, va.at[x, spot(-1)], me.at(dz=1))
    down = v_ring.start(v_ref, va.at[x, spot(1)], me.at(dz=-1))
    for d in (2, 1, 3):
        cross[d, 0].start(v_ref, va.at[x, 0], me.at(dx=d))

    def spread(first, last):
        block = va.at[x, first:last]
        for d in (2, 1, 3):
            cross[d, (first + 1) // 2].start(block, block, me.at(dx=d))

    halves = (slice(0, 2), slice(2, 4))
    k_up = []
    k_down = []

    def k_first():
        own[0].wait()
        for copy in k_side:
            copy.wait_recv()
        for half in halves:
            block = ka.at[half, here]
            k_up.append(k_ring.start(block, block, me.at(dz=1)))
            k_down.append(k_ring.start(block, block, me.at(dz=-1)))

    def k_step(step):
        for n, half in enumerate(halves):
            if step < 4 or n == 0:
                k_up[n].wait_recv()
            if step < 3 or (step == 3 and n == 0):
                block = ka.at[half, me.zs(-step)]
                k_up[n] = k_ring.start(block, block, me.at(dz=1))
            if step < 4 or n == 1:
                k_down[n].wait_recv()
            if step < 3 or (step == 3 and n == 1):
                block = ka.at[half, me.zs(step)]
                k_down[n] = k_ring.start(block, block, me.at(dz=-1))

    def v_step(up, down, step):
        up.wait_recv()
        down.wait_recv()
        if step < 3:
            up = v_ring.start(va.at[x, spot(-step)], va.at[x, spot(-step - 1)], me.at(dz=1))
            down = v_ring.start(va.at[x, spot(step)], va.at[x, spot(step + 1)], me.at(dz=-1))
        elif step == 3:
            low, high = slice(0, 64), slice(64, SUB)
            up = v_ring.start(va.at[x, spot(-3), low], va.at[x, spot(4), low], me.at(dz=1))
            down = v_ring.start(va.at[x, spot(3), high], va.at[x, spot(4), high], me.at(dz=-1))
        if step < 4:
            spread(2 * step - 1, 2 * step + 1)
        else:
            spread(7, 8)
        return up, down

    def make_rows():
        for copy in own[2:]:
            copy.wait()
        deltas = []
        for h in range(HEADS):
            lanes = slice(h * SUB, (h + 1) * SUB)
            product = o_in[:, lanes].astype(F32) * mine[SUB : 2 * SUB, lanes].astype(F32)
            deltas.append(jnp.sum(product.T, axis=0, keepdims=True))
        zero = jnp.zeros((2, SUB), BF16)
        for h in range(HEADS):
            lse_parts = pieces(lse_in[h : h + 1, :] * (-1.0 / SCALE))
            delta_parts = pieces(-deltas[h])
            mine[2 * SUB : 2 * SUB + 16, h * SUB : (h + 1) * SUB] = jnp.concatenate(
                lse_parts + delta_parts + [zero] * 5, axis=0
            )

    q_rows = {}
    q_far = []
    mirrored = {}

    def send_rows():
        mirrored[0] = pair.start(mine, rows_in.at[core, y], sibling)
        for d in (1, 3):
            q_rows[d] = rows.start(mine, rows_in.at[core, y], me.at(dy=d))

    def relay():
        q_rows[1].wait_recv()
        block = rows_in.at[core, me.ys(-1), 0:SUB]
        q_far.append(rows.start(block, block, me.at(dy=1)))
        q_rows[3].wait_recv()
        block = rows_in.at[core, me.ys(1), SUB : 2 * SUB + 16]
        q_far.append(rows.start(block, block, me.at(dy=-1)))

    def mirror(d):
        if d == 2:
            for copy in q_far:
                copy.wait_recv()
        block = rows_in.at[core, me.ys(-d)]
        mirrored[d] = pair.start(block, block, sibling)

    lane, low_cu, high_cu = doc_bounds(cu_ref)
    sub = lax.broadcasted_iota(jnp.int32, (SUB, 1), 0)

    def stack(d):
        mirrored[d].wait_recv()
        a = me.ys(-d)
        for c in range(2):
            row = x * 4 + z // 4 * 2 + c
            qpos = (a * 16 + row) * TILE + z % 4 * SUB + sub
            inside = (qpos >= low_cu) & (qpos < high_cu)
            doc_feat = jnp.where(inside | (lane < 16) | (lane >= 22), 0.0, -16384.0)
            for h in range(HEADS):
                lanes = slice(h * SUB, (h + 1) * SUB)
                to = slice(c * COLS + h * SUB, c * COLS + (h + 1) * SUB)
                qs[a, to, 0:128] = rows_in[c, a, 0:SUB, lanes]
                gs[a, to, 0:128] = rows_in[c, a, SUB : 2 * SUB, lanes]
                stat = rows_in[c, a, 2 * SUB : 2 * SUB + 16, lanes].astype(F32)
                stat = jnp.concatenate([stat, jnp.zeros((SUB - 16, SUB), F32)], axis=0).T
                lse_feat = jnp.where(lane < 3, stat, 0.0)
                delta_feat = jnp.where((lane >= 3) & (lane < 6), stat, 0.0)
                qs[a, to, 128:256] = (lse_feat + doc_feat).astype(BF16)
                gs[a, to, 128:256] = delta_feat.astype(BF16)

    i0 = x * 4 + z // 4 * 2
    zl = z % 4
    ones = lane < 6

    def key_base(b, jj):
        return (b * 16 + 4 * y + jj) * TILE + core * SUB

    def make_feats(kt, carry):
        for zh in range(2):
            pos = key_base(kt // 4, kt % 4) + zh * 2 * SUB + sub
            feats[kt, zh * SUB : (zh + 1) * SUB, :] = (
                (((pos >= low_cu) & (pos < high_cu)) | ones).astype(F32).astype(BF16)
            )
        return carry

    make_rows()
    send_rows()
    k_first()
    lax.fori_loop(0, 16, make_feats, 0)
    dqa[...] = jnp.zeros_like(dqa)
    up, down = v_step(up, down, 1)
    k_step(1)
    up, down = v_step(up, down, 2)
    stack_own = pltpu.make_async_copy(mine, rows_in.at[core, y], own_sem.at[6])
    stack_own.start()
    k_step(2)
    relay()
    mirror(1)
    mirror(3)
    up, down = v_step(up, down, 3)
    stack_own.wait()
    stack(0)
    v_step(up, down, 4)
    k_step(3)
    stack(1)
    stack(3)
    mirror(2)
    stack(2)
    own[1].wait()

    def cross_wait(n, first, last):
        for d in (1, 3, 2):
            whole = cross[d, n].copy(va.at[x, first:last], va.at[me.xs(-d), first:last], me.at(dx=d))
            whole.wait_recv()

    def tile_step(t, carry):
        g = t // 4
        n = (2 + g) % 4
        dx = (t + 1) % 4
        b = (x + dx) % 4
        jj = (zl + n) % 4
        kt = b * 4 + jj

        @pl.when(t == 0)
        def _():
            cross_wait(2, 3, 5)

        @pl.when(t == 4)
        def _():
            cross_wait(1, 1, 3)
            cross_wait(3, 5, 7)
            k_step(4)
            cross_wait(0, 0, 1)
            cross_wait(4, 7, 8)

        near = 2 * n - 1 + (3 - n) // 3
        far = 8 - 2 * n - n // 4
        far = far - (3 - n) // 3
        swap = (z + n) % 8 // 4
        v_first = near + (far - near) * swap
        v_second = far + (near - far) * swap
        keys = ka[b, pl.ds(2 * jj, 2)].reshape(2 * SUB, HEAD_DIM)
        vals = jnp.concatenate([va[b, v_first], va[b, v_second]], axis=0)
        own_tile = t % 4 // 3
        slot = 4 + (g - 4) * own_tile
        r = 4 * y + jj - i0
        acc[slot] = jnp.zeros((2, 2 * SUB, HEAD_DIM), F32)

        def unit(a, count, masked):
            wide = count * 2 * COLS
            many = pl.ds(a, count)
            feat = feats[kt]
            scores = lax.dot_general(
                jnp.concatenate([keys, feat], axis=1),
                qs[many].reshape(wide, 2 * HEAD_DIM),
                LANE,
                preferred_element_type=F32,
            )
            weights = jnp.exp2(scores * (SCALE * LOG2E))
            if masked:
                first = (a * 16 + i0) * TILE + zl * SUB
                kpos = lax.broadcasted_iota(jnp.int32, (2 * SUB, SUB), 0)
                kpos = jnp.where(kpos >= SUB, kpos + SUB, kpos) + key_base(b, jj)
                keep = [kpos <= first + lane, kpos <= first + TILE + lane]
                weights = jnp.concatenate(
                    [
                        jnp.where(keep[m // HEADS], weights[:, m * SUB : (m + 1) * SUB], 0.0)
                        for m in range(2 * HEADS)
                    ],
                    axis=1,
                )
            probs = lax.dot_general(
                jnp.concatenate([vals, feat], axis=1),
                gs[many].reshape(wide, 2 * HEAD_DIM),
                LANE,
                preferred_element_type=F32,
            )
            dscores = (weights * probs).astype(BF16)
            weights = weights.astype(BF16)
            g_rows = gs[many, :, 0:HEAD_DIM].reshape(wide, HEAD_DIM)
            q_all = qs[many, :, 0:HEAD_DIM].reshape(wide, HEAD_DIM)
            acc[slot, 0] += jnp.dot(dscores, q_all, preferred_element_type=F32)
            acc[slot, 1] += jnp.dot(weights, g_rows, preferred_element_type=F32)
            for m in range(count):
                dqa[a + m] += lax.dot_general(
                    keys,
                    dscores[:, m * 2 * COLS : (m + 1) * 2 * COLS],
                    ROW,
                    preferred_element_type=F32,
                )

        ahead = (r >= 0).astype(jnp.int32)
        start = b + ahead

        @pl.when(start <= 2)
        def _():
            unit(start, 2, False)

        @pl.when((start == 3) | ((r >= 0) & (r <= 1)))
        def _():
            single = jnp.where(start == 3, 3, b)
            unit(single, 1, True)

        @pl.when((start == 3) & (r >= 0) & (r <= 1))
        def _():
            unit(b, 1, True)

        @pl.when(own_tile == 0)
        def _():
            for zh in range(2):
                part = slice(zh * SUB, (zh + 1) * SUB)
                stage[t, zh, 0] = (acc[4, 0, part] * SCALE).astype(BF16)
                stage[t, zh, 1] = acc[4, 1, part].astype(BF16)
            side_copy(t, dx).start()

        @pl.when((t > 4) & (t % 4 == 1))
        def _():
            z_start(g - 1)

        return carry

    def side_copy(t, dx):
        return pltpu.make_async_remote_copy(
            src_ref=stage.at[t],
            dst_ref=side_in.at[t],
            send_sem=send_s.at[t],
            recv_sem=recv_s.at[t],
            device_id=me.at(dx=dx),
            device_id_type=MESH,
        )

    def z_copy(g, dz):
        return pltpu.make_async_remote_copy(
            src_ref=z_send.at[g, (z + dz) % 8 // 4],
            dst_ref=z_in.at[dz],
            send_sem=send_z.at[dz],
            recv_sem=recv_z.at[dz],
            device_id=me.at(dz=dz),
            device_id_type=MESH,
        )

    def z_start(g):
        n = (2 + g) % 4
        for e in range(3):
            side_copy(4 * g + e, e + 1).wait_recv()
        for zh in range(2):
            part = slice(zh * SUB, (zh + 1) * SUB)
            for kv in range(2):
                total = acc[g, kv, part] * (SCALE if kv == 0 else 1.0)
                for e in range(3):
                    total += side_in[4 * g + e, zh, kv].astype(F32)
                z_send[g, zh, kv] = total.astype(BF16)

        @pl.when(n > 0)
        def _():
            z_copy(g, n).start()

        z_copy(g, n + 4).start()

    lax.fori_loop(0, 16, tile_step, 0)

    for c in range(2):
        for a in range(4):
            for h in range(HEADS):
                lanes = slice(h * SUB, (h + 1) * SUB)
                to = slice(c * COLS + h * SUB, c * COLS + (h + 1) * SUB)
                dq_low[c, a, :, lanes] = (dqa[a, :, to].T * SCALE).astype(BF16)
    last = Sender(send_d, recv_d)
    swap_copy = last.start(dq_low.at[1 - core], q_pair, sibling)
    z_start(3)
    swap_copy.wait_recv()
    q_back = []
    for d in (2, 1, 3):
        a = me.ys(d)
        q_send[d - 1] = (dq_low[core, a].astype(F32) + q_pair[a].astype(F32)).astype(BF16)
        q_back.append(last.start(q_send.at[d - 1], q_in.at[d - 1], me.at(dy=d)))
    for dz in (2, 6, 3, 7, 4, 1, 5):
        z_copy((dz + 2) % 4, dz).wait_recv()
    for kv in range(2):
        total = z_send[2, z // 4, kv].astype(F32)
        for dz in range(1, 8):
            total += z_in[dz, kv].astype(F32)
        lanes = slice(COLS + kv * HEAD_DIM, COLS + (kv + 1) * HEAD_DIM)
        all_out[:, lanes] = total.astype(BF16)
    total = dq_low[core, y].astype(F32) + q_pair[y].astype(F32)
    for copy in q_back:
        copy.wait_recv()
    for m in range(3):
        total += q_in[m].astype(F32)
    all_out[:, 0:COLS] = total.astype(BF16)

    rows.finish(rows_in.at[0, 0:3], sibling)
    pair.finish(rows_in.at[0], sibling)
    v_ring.finish(va.at[x, 0:7], sibling)
    k_ring.finish(ka.at[0:4, 0:7], sibling)
    k_cross.finish()
    for n, first, size in ((0, 0, 1), (1, 1, 2), (2, 3, 2), (3, 5, 2), (4, 7, 1)):
        for d in (1, 2, 3):
            block = va.at[x, first : first + size]
            cross[d, n].copy(block, block, me.at(dx=d)).wait_send()
    for g in range(4):
        for e in range(3):
            side_copy(4 * g + e, e + 1).wait_send()
    for dz in range(1, 8):
        z_copy((dz + 2) % 4, dz).wait_send()
    last.finish()


def grads(cu, q, g, k, v, o, lse):
    dma = pltpu.SemaphoreType.DMA
    block = (SUB, HEAD_DIM)
    message = (2 * SUB + 16, COLS)
    vmem = pltpu.VMEM
    return pl.pallas_call(
        grads_kernel,
        out_shape=jax.ShapeDtypeStruct((SUB, COLS + 2 * HEAD_DIM), BF16),
        in_specs=[pl.BlockSpec(memory_space=pltpu.SMEM)] + [ANY] * 6,
        out_specs=VMEM,
        scratch_shapes=[
            vmem((4, 8) + block, BF16),
            vmem((4, 8) + block, BF16),
            vmem((2, 4) + message, BF16),
            vmem(message, BF16),
            vmem((4, 2 * COLS, 2 * HEAD_DIM), BF16),
            vmem((4, 2 * COLS, 2 * HEAD_DIM), BF16),
            vmem((SUB, COLS), BF16),
            vmem((HEADS, SUB), F32),
            vmem((16, 2 * SUB, HEAD_DIM), BF16),
            vmem((5, 2, 2 * SUB, HEAD_DIM), F32),
            vmem((4, HEAD_DIM, 2 * COLS), F32),
            vmem((16, 2, 2) + block, BF16),
            vmem((16, 2, 2) + block, BF16),
            vmem((4, 2, 2) + block, BF16),
            vmem((8, 2) + block, BF16),
            vmem((8, 128), F32),
            vmem((2, 4, SUB, COLS), BF16),
            vmem((4, SUB, COLS), BF16),
            vmem((3, SUB, COLS), BF16),
            vmem((3, SUB, COLS), BF16),
            dma((4,)),
            dma((4,)),
            dma((8,)),
            dma((14,)),
            dma((3, 5)),
            dma((3, 5)),
            dma((3,)),
            dma((3,)),
            dma((4,)),
            dma((7,)),
            dma((16,)),
            dma((16,)),
            dma((8,)),
            dma((8,)),
            dma((4,)),
            dma((4,)),
        ],
        compiler_params=pltpu.CompilerParams(
            collective_id=0, has_side_effects=True, vmem_limit_bytes=63 * 1024 * 1024
        ),
        name="grads",
    )(cu, q, g, k, v, o, lse)


def split_kernel(all_ref, dq_ref, dk_ref, dv_ref):
    dq_ref[...] = all_ref[:, 0:COLS]
    dk_ref[...] = all_ref[:, COLS : COLS + HEAD_DIM]
    dv_ref[...] = all_ref[:, COLS + HEAD_DIM : COLS + 2 * HEAD_DIM]


def split(grads):
    return pl.pallas_call(
        split_kernel,
        out_shape=[
            jax.ShapeDtypeStruct((SUB, COLS), BF16),
            jax.ShapeDtypeStruct((SUB, HEAD_DIM), BF16),
            jax.ShapeDtypeStruct((SUB, HEAD_DIM), BF16),
        ],
        in_specs=[VMEM],
        out_specs=[VMEM] * 3,
        name="split",
    )(grads)


def per_device(query, keys, values, out, out_grad, lse, cu_seqlens, tile_table):
    return split(grads(cu_seqlens, query, out_grad, keys, values, out, lse))


def solution(mesh):
    placed = (
        P(("qrow", "kcol"), None),
        P(("kcol", "qrow"), None),
        P(("kcol", "qrow"), None),
        P(("qrow", "kcol"), None),
        P(("qrow", "kcol"), None),
        P(None, ("qrow", "kcol")),
        P(),
        P("qrow", "kcol", None),
    )
    return jax.shard_map(
        per_device,
        mesh=mesh,
        in_specs=placed,
        out_specs=(P(("qrow", "kcol"), None), P(("kcol", "qrow"), None), P(("kcol", "qrow"), None)),
        check_vma=False,
    )
```

time: 649 us -> 74.3 us (0.11)
  the two profiles are of different devices: /device:TPU:33 before, /device:TPU:80 now
where the time goes in v3:
time: 74.3 us; the launch traced here: 74.2 us
  Pallas kernels  73.5 us (99%)
    pallas_call x1, Pallas kernels, grads(): pl.pallas_call(grads_kernel, out_shape=jax.ShapeDtypeStruct((SUB, COLS +...  71.9 us
    pallas_call x1, Pallas kernels, split(): pl.pallas_call(split_kernel, out_shape=[jax.ShapeDtypeStruct((SUB, COLS),...  1.61 us

profile of v3, /device:TPU:80, one launch (start us, length us, event | category | flops | bytes accessed | tf_op | source)
XLA Modules:
  0.0 74.2 jit_solution(12244911461911191417)
XLA Ops:
  0.6 71.9 %grads.1.all_ref = bf16[128,768]{1,0:T(8,128)(2,1)} custom-call(s32[7]{0:T(128)} %cu_ref.1, bf16[128,512]{1,0:T(8,128)(2,1)} %q_ref.1, bf16[128,512]{1,0:T(8,128)(2,1)} %g_ref.1, bf16[128,128]{1,0:T(8,128)(2,1)} %k_ref.1, bf16[128,128]{1,0:T(8,128)(2,1)} %v_ref.1, bf16[128,512]{1,0:T(8,128)(2,1)} %o_ref.1, f32[4,128]{1,0:T(4,128)} %lse_ref.1), custom_call_target="tpu_custom_call" | custom-call | tf_op jit(solution)/shard_map/grads/pallas_call | solution.py:556
  72.6 1.6 %split.1 = (bf16[128,512]{1,0:T(8,128)(2,1)}, bf16[128,128]{1,0:T(8,128)(2,1)}, bf16[128,128]{1,0:T(8,128)(2,1)}) custom-call(bf16[128,768]{1,0:T(8,128)(2,1)} %grads.1.all_ref), custom_call_target="tpu_custom_call" | custom-call | tf_op jit(solution)/shard_map/split/pallas_call | solution.py:613

commit v4 on v3

--- a/solution.py
+++ b/solution.py
@@ -164,7 +164,7 @@
 
 def grads_kernel(
     cu_ref, q_ref, g_ref, k_ref, v_ref, o_ref, lse_ref, all_out, ka, va, rows_in, mine, qs, gs, o_in, lse_in, feats, acc, dqa,
-    stage, side_in, z_send, z_in, kept, dq_low, q_pair, q_send, q_in,
+    stage, side_in, z_send, z_in, dq_low, q_pair, q_send, q_in,
     recv_q, recv_m, recv_v, recv_k, send_x, recv_x, send_k, recv_kx, send_all, own_sem, send_s, recv_s, send_z, recv_z, send_d, recv_d
 ):
     me = Place()
@@ -195,8 +195,7 @@
     k_cross = Sender(send_k, recv_kx)
     cross = {(d, n): Batch(send_x.at[d - 1, n], recv_x.at[d - 1, n]) for d in (1, 2, 3) for n in range(5)}
     k_side = [k_cross.start(k_ref, ka.at[x, here], me.at(dx=d)) for d in (2, 1, 3)]
-    up = v_ring.start(v_ref, va.at[x, spot(-1)], me.at(dz=1))
-    down = v_ring.start(v_ref, va.at[x, spot(1)], me.at(dz=-1))
+    v_in = {d: v_ring.start(v_ref, va.at[x, spot(-d)], me.at(dz=d)) for d in (1, -1, 2, -2, 3, -3, 4)}
     for d in (2, 1, 3):
         cross[d, 0].start(v_ref, va.at[x, 0], me.at(dx=d))
 
@@ -231,21 +230,13 @@
                 block = ka.at[half, me.zs(step)]
                 k_down[n] = k_ring.start(block, block, me.at(dz=-1))
 
-    def v_step(up, down, step):
-        up.wait_recv()
-        down.wait_recv()
-        if step < 3:
-            up = v_ring.start(va.at[x, spot(-step)], va.at[x, spot(-step - 1)], me.at(dz=1))
-            down = v_ring.start(va.at[x, spot(step)], va.at[x, spot(step + 1)], me.at(dz=-1))
-        elif step == 3:
-            low, high = slice(0, 64), slice(64, SUB)
-            up = v_ring.start(va.at[x, spot(-3), low], va.at[x, spot(4), low], me.at(dz=1))
-            down = v_ring.start(va.at[x, spot(3), high], va.at[x, spot(4), high], me.at(dz=-1))
+    def v_step(step):
+        v_in[step].wait_recv()
         if step < 4:
+            v_in[-step].wait_recv()
             spread(2 * step - 1, 2 * step + 1)
         else:
             spread(7, 8)
-        return up, down
 
     def make_rows():
         for copy in own[2:]:
@@ -327,26 +318,26 @@
 
     make_rows()
     send_rows()
+    stack_own = pltpu.make_async_copy(mine, rows_in.at[core, y], own_sem.at[6])
+    stack_own.start()
     k_first()
+    v_step(1)
     lax.fori_loop(0, 16, make_feats, 0)
     dqa[...] = jnp.zeros_like(dqa)
-    up, down = v_step(up, down, 1)
+    v_step(2)
     k_step(1)
-    up, down = v_step(up, down, 2)
-    stack_own = pltpu.make_async_copy(mine, rows_in.at[core, y], own_sem.at[6])
-    stack_own.start()
-    k_step(2)
+    v_step(3)
+    v_step(4)
     relay()
     mirror(1)
     mirror(3)
-    up, down = v_step(up, down, 3)
     stack_own.wait()
     stack(0)
-    v_step(up, down, 4)
-    k_step(3)
+    k_step(2)
     stack(1)
     stack(3)
     mirror(2)
+    k_step(3)
     stack(2)
     own[1].wait()
 
@@ -431,6 +422,32 @@
                     preferred_element_type=F32,
                 )
 
+        def half_unit(a):
+            feat = feats[kt]
+            q_half = qs[a, COLS : 2 * COLS]
+            g_half = gs[a, COLS : 2 * COLS]
+            scores = lax.dot_general(
+                jnp.concatenate([keys, feat], axis=1), q_half, LANE, preferred_element_type=F32
+            )
+            weights = jnp.exp2(scores * (SCALE * LOG2E))
+            kpos = lax.broadcasted_iota(jnp.int32, (2 * SUB, SUB), 0)
+            kpos = jnp.where(kpos >= SUB, kpos + SUB, kpos)
+            keep = kpos + core * SUB <= zl * SUB + lane
+            weights = jnp.concatenate(
+                [jnp.where(keep, weights[:, m * SUB : (m + 1) * SUB], 0.0) for m in range(HEADS)],
+                axis=1,
+            )
+            probs = lax.dot_general(
+                jnp.concatenate([vals, feat], axis=1), g_half, LANE, preferred_element_type=F32
+            )
+            dscores = (weights * probs).astype(BF16)
+            weights = weights.astype(BF16)
+            acc[slot, 0] += jnp.dot(dscores, q_half[:, 0:HEAD_DIM], preferred_element_type=F32)
+            acc[slot, 1] += jnp.dot(weights, g_half[:, 0:HEAD_DIM], preferred_element_type=F32)
+            dqa[a, :, COLS : 2 * COLS] += lax.dot_general(
+                keys, dscores, ROW, preferred_element_type=F32
+            )
+
         ahead = (r >= 0).astype(jnp.int32)
         start = b + ahead
 
@@ -438,14 +455,15 @@
         def _():
             unit(start, 2, False)
 
-        @pl.when((start == 3) | ((r >= 0) & (r <= 1)))
+        def single(u, carry):
+            unit(jnp.where(u == 0, 3, b), 1, True)
+            return carry
+
+        lax.fori_loop(jnp.where(start == 3, 0, 1), jnp.where(r == 0, 2, 1), single, 0)
+
+        @pl.when(r == 1)
         def _():
-            single = jnp.where(start == 3, 3, b)
-            unit(single, 1, True)
-
-        @pl.when((start == 3) & (r >= 0) & (r <= 1))
-        def _():
-            unit(b, 1, True)
+            half_unit(b)
 
         @pl.when(own_tile == 0)
         def _():
@@ -455,7 +473,7 @@
                 stage[t, zh, 1] = acc[4, 1, part].astype(BF16)
             side_copy(t, dx).start()
 
-        @pl.when((t > 4) & (t % 4 == 1))
+        @pl.when((t > 4) & (t % 4 == 3))
         def _():
             z_start(g - 1)
 
@@ -501,21 +519,35 @@
 
     lax.fori_loop(0, 16, tile_step, 0)
 
-    for c in range(2):
-        for a in range(4):
+    last = Sender(send_d, recv_d)
+    swaps = {}
+
+    def dq_swap(d):
+        a = me.ys(d)
+        for c in range(2):
             for h in range(HEADS):
                 lanes = slice(h * SUB, (h + 1) * SUB)
                 to = slice(c * COLS + h * SUB, c * COLS + (h + 1) * SUB)
                 dq_low[c, a, :, lanes] = (dqa[a, :, to].T * SCALE).astype(BF16)
-    last = Sender(send_d, recv_d)
-    swap_copy = last.start(dq_low.at[1 - core], q_pair, sibling)
-    z_start(3)
-    swap_copy.wait_recv()
+        swaps[d] = last.start(dq_low.at[1 - core, a], q_pair.at[a], sibling)
+
     q_back = []
-    for d in (2, 1, 3):
+
+    def dq_send(d):
         a = me.ys(d)
+        swaps[d].wait_recv()
         q_send[d - 1] = (dq_low[core, a].astype(F32) + q_pair[a].astype(F32)).astype(BF16)
         q_back.append(last.start(q_send.at[d - 1], q_in.at[d - 1], me.at(dy=d)))
+
+    dq_swap(2)
+    dq_swap(1)
+    dq_swap(3)
+    dq_send(2)
+    dq_send(1)
+    dq_send(3)
+    z_start(3)
+    dq_swap(0)
+    swaps[0].wait_recv()
     for dz in (2, 6, 3, 7, 4, 1, 5):
         z_copy((dz + 2) % 4, dz).wait_recv()
     for kv in range(2):
@@ -574,7 +606,6 @@
             vmem((16, 2, 2) + block, BF16),
             vmem((4, 2, 2) + block, BF16),
             vmem((8, 2) + block, BF16),
-            vmem((8, 128), F32),
             vmem((2, 4, SUB, COLS), BF16),
             vmem((4, SUB, COLS), BF16),
             vmem((3, SUB, COLS), BF16),
@@ -593,8 +624,8 @@
             dma((16,)),
             dma((8,)),
             dma((8,)),
-            dma((4,)),
-            dma((4,)),
+            dma((7,)),
+            dma((7,)),
         ],
         compiler_params=pltpu.CompilerParams(
             collective_id=0, has_side_effects=True, vmem_limit_bytes=63 * 1024 * 1024

time: 74.3 us -> 67.4 us (0.907)
  the two profiles are of different devices: /device:TPU:80 before, /device:TPU:33 now
where the time goes in v4:
time: 67.4 us; the launch traced here: 67.3 us
  Pallas kernels  66.7 us (99%)
    pallas_call x1, Pallas kernels, grads(): pl.pallas_call(grads_kernel, out_shape=jax.ShapeDtypeStruct((SUB, COLS +...  65.1 us
    pallas_call x1, Pallas kernels, split(): pl.pallas_call(split_kernel, out_shape=[jax.ShapeDtypeStruct((SUB, COLS),...  1.61 us

profile of v4, /device:TPU:33, one launch (start us, length us, event | category | flops | bytes accessed | tf_op | source)
XLA Modules:
  0.0 67.3 jit_solution(10993235005956461211)
XLA Ops:
  0.6 65.1 %grads.1.all_ref = bf16[128,768]{1,0:T(8,128)(2,1)} custom-call(s32[7]{0:T(128)} %cu_ref.1, bf16[128,512]{1,0:T(8,128)(2,1)} %q_ref.1, bf16[128,512]{1,0:T(8,128)(2,1)} %g_ref.1, bf16[128,128]{1,0:T(8,128)(2,1)} %k_ref.1, bf16[128,128]{1,0:T(8,128)(2,1)} %v_ref.1, bf16[128,512]{1,0:T(8,128)(2,1)} %o_ref.1, f32[4,128]{1,0:T(4,128)} %lse_ref.1), custom_call_target="tpu_custom_call" | custom-call | tf_op jit(solution)/shard_map/grads/pallas_call | solution.py:588
  65.7 1.6 %split.1 = (bf16[128,512]{1,0:T(8,128)(2,1)}, bf16[128,128]{1,0:T(8,128)(2,1)}, bf16[128,128]{1,0:T(8,128)(2,1)}) custom-call(bf16[128,768]{1,0:T(8,128)(2,1)} %grads.1.all_ref), custom_call_target="tpu_custom_call" | custom-call | tf_op jit(solution)/shard_map/split/pallas_call | solution.py:644

commit v5 on v4

--- a/solution.py
+++ b/solution.py
@@ -193,7 +193,20 @@
     v_ring = Lane(send_all.at[2], recv_v)
     k_ring = Lane(send_all.at[3], recv_k)
     k_cross = Sender(send_k, recv_kx)
+    q_part, g_part, s_part = slice(0, SUB), slice(SUB, 2 * SUB), slice(2 * SUB, 2 * SUB + 16)
+    mirrored = {}
+    q_rows = {1: [], 2: [], 3: []}
+
+    def send_rows():
+        for n in range(2):
+            for d, part, src in ((1, q_part, q_ref), (3, g_part, g_ref)) if n == 0 else (
+                (1, g_part, g_ref),
+                (3, q_part, q_ref),
+            ):
+                q_rows[d].append(rows.start(src, rows_in.at[core, y, part], me.at(dy=d)))
+
     cross = {(d, n): Batch(send_x.at[d - 1, n], recv_x.at[d - 1, n]) for d in (1, 2, 3) for n in range(5)}
+    send_rows()
     k_side = [k_cross.start(k_ref, ka.at[x, here], me.at(dx=d)) for d in (2, 1, 3)]
     v_in = {d: v_ring.start(v_ref, va.at[x, spot(-d)], me.at(dz=d)) for d in (1, -1, 2, -2, 3, -3, 4)}
     for d in (2, 1, 3):
@@ -219,16 +232,12 @@
 
     def k_step(step):
         for n, half in enumerate(halves):
-            if step < 4 or n == 0:
-                k_up[n].wait_recv()
-            if step < 3 or (step == 3 and n == 0):
-                block = ka.at[half, me.zs(-step)]
-                k_up[n] = k_ring.start(block, block, me.at(dz=1))
-            if step < 4 or n == 1:
-                k_down[n].wait_recv()
-            if step < 3 or (step == 3 and n == 1):
-                block = ka.at[half, me.zs(step)]
-                k_down[n] = k_ring.start(block, block, me.at(dz=-1))
+            k_up[n].wait_recv()
+            block = ka.at[half, me.zs(-step)]
+            k_up[n] = k_ring.start(block, block, me.at(dz=1))
+            k_down[n].wait_recv()
+            block = ka.at[half, me.zs(step)]
+            k_down[n] = k_ring.start(block, block, me.at(dz=-1))
 
     def v_step(step):
         v_in[step].wait_recv()
@@ -254,27 +263,22 @@
                 lse_parts + delta_parts + [zero] * 5, axis=0
             )
 
-    q_rows = {}
-    q_far = []
-    mirrored = {}
-
-    def send_rows():
+    def send_stats():
+        for d in (1, 3, 2):
+            q_rows[d].append(rows.start(mine.at[s_part], rows_in.at[core, y, s_part], me.at(dy=d)))
         mirrored[0] = pair.start(mine, rows_in.at[core, y], sibling)
-        for d in (1, 3):
-            q_rows[d] = rows.start(mine, rows_in.at[core, y], me.at(dy=d))
 
     def relay():
-        q_rows[1].wait_recv()
-        block = rows_in.at[core, me.ys(-1), 0:SUB]
-        q_far.append(rows.start(block, block, me.at(dy=1)))
-        q_rows[3].wait_recv()
-        block = rows_in.at[core, me.ys(1), SUB : 2 * SUB + 16]
-        q_far.append(rows.start(block, block, me.at(dy=-1)))
+        q_rows[1][0].wait_recv()
+        block = rows_in.at[core, me.ys(-1), q_part]
+        q_rows[2].append(rows.start(block, block, me.at(dy=1)))
+        q_rows[3][0].wait_recv()
+        block = rows_in.at[core, me.ys(1), g_part]
+        q_rows[2].append(rows.start(block, block, me.at(dy=-1)))
 
     def mirror(d):
-        if d == 2:
-            for copy in q_far:
-                copy.wait_recv()
+        for copy in q_rows[d] if d == 2 else q_rows[d][1:]:
+            copy.wait_recv()
         block = rows_in.at[core, me.ys(-d)]
         mirrored[d] = pair.start(block, block, sibling)
 
@@ -317,29 +321,49 @@
         return carry
 
     make_rows()
-    send_rows()
+    send_stats()
     stack_own = pltpu.make_async_copy(mine, rows_in.at[core, y], own_sem.at[6])
     stack_own.start()
     k_first()
     v_step(1)
+    relay()
     lax.fori_loop(0, 16, make_feats, 0)
     dqa[...] = jnp.zeros_like(dqa)
     v_step(2)
-    k_step(1)
     v_step(3)
     v_step(4)
-    relay()
     mirror(1)
     mirror(3)
+    k_step(1)
     stack_own.wait()
     stack(0)
-    k_step(2)
+    mirror(2)
     stack(1)
     stack(3)
-    mirror(2)
-    k_step(3)
+    k_step(2)
     stack(2)
     own[1].wait()
+
+    def k_last(n):
+        block = ka.at[halves[n], me.zs(-3 if n == 0 else 3)]
+        return pltpu.make_async_remote_copy(
+            src_ref=block,
+            dst_ref=block,
+            send_sem=send_all.at[3],
+            recv_sem=recv_k.at[12 + n],
+            device_id=me.at(dz=1 if n == 0 else -1),
+            device_id_type=MESH,
+        )
+
+    def k_third():
+        for n in range(2):
+            k_up[n].wait_recv()
+            k_down[n].wait_recv()
+            k_last(n).start()
+
+    def k_fourth():
+        for n in range(2):
+            k_last(n).wait_recv()
 
     def cross_wait(n, first, last):
         for d in (1, 3, 2):
@@ -358,11 +382,18 @@
         def _():
             cross_wait(2, 3, 5)
 
+        @pl.when(t == 2)
+        def _():
+            k_third()
+
         @pl.when(t == 4)
         def _():
             cross_wait(1, 1, 3)
             cross_wait(3, 5, 7)
-            k_step(4)
+
+        @pl.when(t == 8)
+        def _():
+            k_fourth()
             cross_wait(0, 0, 1)
             cross_wait(4, 7, 8)
 
@@ -610,7 +641,7 @@
             vmem((4, SUB, COLS), BF16),
             vmem((3, SUB, COLS), BF16),
             vmem((3, SUB, COLS), BF16),
-            dma((4,)),
+            dma((9,)),
             dma((4,)),
             dma((8,)),
             dma((14,)),

time: 67.4 us -> 64.3 us (0.954)
  Pallas kernels: 66.7 us -> 63.5 us
    pallas_call x1, Pallas kernels: 65.1 us -> 61.9 us  [grads(): pl.pallas_call(grads_kernel, out_shape=jax.ShapeDtypeStruct((SUB, COLS +...]
where the time goes in v5:
time: 64.3 us; the launch traced here: 64.2 us
  Pallas kernels  63.5 us (99%)
    pallas_call x1, Pallas kernels, grads(): pl.pallas_call(grads_kernel, out_shape=jax.ShapeDtypeStruct((SUB, COLS +...  61.9 us
    pallas_call x1, Pallas kernels, split(): pl.pallas_call(split_kernel, out_shape=[jax.ShapeDtypeStruct((SUB, COLS),...  1.61 us

profile of v5, /device:TPU:33, one launch (start us, length us, event | category | flops | bytes accessed | tf_op | source)
XLA Modules:
  0.0 64.2 jit_solution(7303767116496437524)
XLA Ops:
  0.6 61.9 %grads.1.all_ref = bf16[128,768]{1,0:T(8,128)(2,1)} custom-call(s32[7]{0:T(128)} %cu_ref.1, bf16[128,512]{1,0:T(8,128)(2,1)} %q_ref.1, bf16[128,512]{1,0:T(8,128)(2,1)} %g_ref.1, bf16[128,128]{1,0:T(8,128)(2,1)} %k_ref.1, bf16[128,128]{1,0:T(8,128)(2,1)} %v_ref.1, bf16[128,512]{1,0:T(8,128)(2,1)} %o_ref.1, f32[4,128]{1,0:T(4,128)} %lse_ref.1), custom_call_target="tpu_custom_call" | custom-call | tf_op jit(solution)/shard_map/grads/pallas_call | solution.py:619
  62.6 1.6 %split.1 = (bf16[128,512]{1,0:T(8,128)(2,1)}, bf16[128,128]{1,0:T(8,128)(2,1)}, bf16[128,128]{1,0:T(8,128)(2,1)}) custom-call(bf16[128,768]{1,0:T(8,128)(2,1)} %grads.1.all_ref), custom_call_target="tpu_custom_call" | custom-call | tf_op jit(solution)/shard_map/split/pallas_call | solution.py:675

commit v6 on v5

--- a/solution.py
+++ b/solution.py
@@ -574,9 +574,9 @@
     dq_swap(1)
     dq_swap(3)
     dq_send(2)
+    z_start(3)
     dq_send(1)
     dq_send(3)
-    z_start(3)
     dq_swap(0)
     swaps[0].wait_recv()
     for dz in (2, 6, 3, 7, 4, 1, 5):

time: 64.3 us -> 63.9 us (level)
  no operation moved by 1% of the time
where the time goes in v6:
time: 63.9 us; the launch traced here: 63.8 us
  Pallas kernels  63.2 us (99%)
  between operations  0.64 us (1%)
    pallas_call x1, Pallas kernels, grads(): pl.pallas_call(grads_kernel, out_shape=jax.ShapeDtypeStruct((SUB, COLS +...  61.5 us
    pallas_call x1, Pallas kernels, split(): pl.pallas_call(split_kernel, out_shape=[jax.ShapeDtypeStruct((SUB, COLS),...  1.61 us

profile of v6, /device:TPU:33, one launch (start us, length us, event | category | flops | bytes accessed | tf_op | source)
XLA Modules:
  0.0 63.8 jit_solution(7430415612361362128)
XLA Ops:
  0.6 61.5 %grads.1.all_ref = bf16[128,768]{1,0:T(8,128)(2,1)} custom-call(s32[7]{0:T(128)} %cu_ref.1, bf16[128,512]{1,0:T(8,128)(2,1)} %q_ref.1, bf16[128,512]{1,0:T(8,128)(2,1)} %g_ref.1, bf16[128,128]{1,0:T(8,128)(2,1)} %k_ref.1, bf16[128,128]{1,0:T(8,128)(2,1)} %v_ref.1, bf16[128,512]{1,0:T(8,128)(2,1)} %o_ref.1, f32[4,128]{1,0:T(4,128)} %lse_ref.1), custom_call_target="tpu_custom_call" | custom-call | tf_op jit(solution)/shard_map/grads/pallas_call | solution.py:619
  62.2 1.6 %split.1 = (bf16[128,512]{1,0:T(8,128)(2,1)}, bf16[128,128]{1,0:T(8,128)(2,1)}, bf16[128,128]{1,0:T(8,128)(2,1)}) custom-call(bf16[128,768]{1,0:T(8,128)(2,1)} %grads.1.all_ref), custom_call_target="tpu_custom_call" | custom-call | tf_op jit(solution)/shard_map/split/pallas_call | solution.py:675
